TPU v7x, 32 devices: a whole 2x2x4 slice. The times are simulated.
32 devices in a mesh: batch: 4 (over y, x), ctx: 8 (over z, core).
Axes of the slice: x: 2, y: 2, z: 4, core: 2. Of those that a mesh axis runs over, the one named last changes fastest.
Arguments:
- tokens: bfloat16 [4, 1536, 960], P('batch', 'ctx'), may hold values from -6 to 6
- attention_weights: bfloat16 [2457600], P(('batch', 'ctx')), may hold values from -2 to 2
- feedforward_weights: bfloat16 [7372800], P(('batch', 'ctx')), may hold values from -1 to 1
- norm_gains: float32 [2, 960], P(None, 'ctx'), may hold values from 0.5 to 1.5
- span_order: int32 [4, 16], P('batch', 'ctx'), may hold values from 0 to 15, as said below
- cotangent: bfloat16 [4, 1536, 960], P('batch', 'ctx'), may hold values from -6 to 6
Outputs:
- out_tokens: bfloat16 [4, 1536, 960], P('batch', 'ctx')
- grad_tokens: float32 [4, 1536, 960], P('batch', 'ctx')
- grad_attention: float32 [2457600], P(('batch', 'ctx'))
- grad_feedforward: float32 [7372800], P(('batch', 'ctx'))
- grad_norm_gains: float32 [2, 960], P(None, 'ctx')
Inputs may be any that keep to these rules, and one draw needn't show every extreme that they name: `span_order`: each row is a permutation of 0 to 15 in which entries 2c and 2c + 1 sum to 15.
All inputs are finite; a program needn't handle non-finite values.
Results may differ from a plain program's by a relative error of at most 0.025.
Values may be sent and summed in bfloat16 or wider, within the bound.
No kernel may reach another device: no remote copies, remote signals or barrier semaphores. Data moves between devices by JAX's collectives and lax.ppermute only.
A program may use at most 192 MiB of HBM per device.

v0:
```python
import math

import jax
import jax.numpy as jnp
from jax import lax
from jax.sharding import PartitionSpec as P

D = 960
HEADS = 15
KV_HEADS = 5
HEAD_DIM = 64
FF = 2560


ROPE_BASE = 100000.0
EPS = 1e-05
NEG = -1e30


def normalize(values, gain):
    return values * lax.rsqrt(jnp.mean(values * values, -1, keepdims=True) + EPS) * gain


def swiglu(gate, upward):
    return jax.nn.silu(gate) * upward


def rope_tables(positions):
    halves = HEAD_DIM // 2
    inverse_freq = ROPE_BASE ** (-jnp.arange(halves, dtype=jnp.float32) / halves)
    angles = positions.astype(jnp.float32)[:, None] * inverse_freq[None, :]
    return (jnp.cos(angles), jnp.sin(angles))


def rotate(values, cos_table, sin_table):
    halves = HEAD_DIM // 2
    first = values[..., :halves]
    second = values[..., halves:]
    cos_table = cos_table[:, None, :]
    sin_table = sin_table[:, None, :]
    return jnp.concatenate(
        [first * cos_table - second * sin_table, second * cos_table + first * sin_table], -1
    )


def split_flat(flat, shapes):
    pieces = []
    offset = 0
    for rows_in, cols_in in shapes:
        pieces.append(flat[offset : offset + rows_in * cols_in].reshape(rows_in, cols_in))
        offset += rows_in * cols_in
    return pieces


def unpack(att_flat, ff_flat):
    width_q = HEADS * HEAD_DIM
    width_kv = KV_HEADS * HEAD_DIM
    att_parts = split_flat(att_flat, [(D, width_q), (D, width_kv), (D, width_kv), (width_q, D)])
    ff_parts = split_flat(ff_flat, [(D, FF), (D, FF), (FF, D)])
    return (att_parts, ff_parts)


def score_block(queries, key_block, query_pos, key_pos):
    keys_three = key_block.reshape(key_block.shape[0], KV_HEADS, HEAD_DIM)
    scores = jnp.einsum(
        "qhgd,khd->hgqk", queries, keys_three, preferred_element_type=jnp.float32
    ) * HEAD_DIM ** (-0.5)
    visible = key_pos[None, None, None, :] <= query_pos[None, None, :, None]
    return (scores, visible)


def attention_forward(queries, key_all, value_all, query_pos, key_pos, block):
    rows_here = queries.shape[0]
    group = HEADS // KV_HEADS
    count = key_all.shape[0] // block
    key_blocks = key_all.reshape(count, block, key_all.shape[1])
    value_blocks = value_all.reshape(count, block, value_all.shape[1])
    pos_blocks = key_pos.reshape(count, block)

    def online_step(carry, item):
        top, total, accum = carry
        key_block, value_block, pos_block = item
        scores, visible = score_block(queries, key_block, query_pos, pos_block)
        scores = jnp.where(visible, scores, NEG)
        new_top = jnp.maximum(top, jnp.max(scores, -1))
        weights = jnp.where(visible, jnp.exp(scores - new_top[..., None]), 0.0)
        factor = jnp.exp(top - new_top)
        total = total * factor + jnp.sum(weights, -1)
        values_three = value_block.reshape(block, KV_HEADS, HEAD_DIM)
        accum = accum * jnp.transpose(factor, (2, 0, 1))[..., None]
        accum = accum + jnp.einsum(
            "hgqk,khd->qhgd",
            weights.astype(jnp.bfloat16),
            values_three,
            preferred_element_type=jnp.float32,
        )
        return ((new_top, total, accum), None)

    start_top = jnp.full((KV_HEADS, group, rows_here), NEG, jnp.float32)
    start_total = jnp.zeros((KV_HEADS, group, rows_here), jnp.float32)
    start_out = jnp.zeros((rows_here, KV_HEADS, group, HEAD_DIM), jnp.float32)
    (top, total, accum), unused = lax.scan(
        online_step, (start_top, start_total, start_out), (key_blocks, value_blocks, pos_blocks)
    )
    log_total = top + jnp.log(total)
    attended = accum / jnp.transpose(total, (2, 0, 1))[..., None]
    return (attended, log_total)


def attention_backward(
    queries, key_all, value_all, query_pos, key_pos, block, log_total, grad_out, attended
):
    rows_here = queries.shape[0]
    group = HEADS // KV_HEADS
    width_kv = key_all.shape[1]
    count = key_all.shape[0] // block
    items = (
        key_all.reshape(count, block, width_kv),
        value_all.reshape(count, block, width_kv),
        key_pos.reshape(count, block),
    )
    delta = jnp.transpose(jnp.sum(grad_out.astype(jnp.float32) * attended, -1), (1, 2, 0))

    def grad_step(grad_query, item):
        key_block, value_block, pos_block = item
        scores, visible = score_block(queries, key_block, query_pos, pos_block)
        probs = jnp.where(visible, jnp.exp(scores - log_total[..., None]), 0.0)
        values_three = value_block.reshape(block, KV_HEADS, HEAD_DIM)
        grad_probs = jnp.einsum(
            "qhgd,khd->hgqk", grad_out, values_three, preferred_element_type=jnp.float32
        )
        grad_scores = (probs * (grad_probs - delta[..., None])).astype(jnp.bfloat16)
        keys_three = key_block.reshape(block, KV_HEADS, HEAD_DIM)
        grad_query = grad_query + jnp.einsum(
            "hgqk,khd->qhgd", grad_scores, keys_three, preferred_element_type=jnp.float32
        )
        grad_key = jnp.einsum(
            "hgqk,qhgd->khd", grad_scores, queries, preferred_element_type=jnp.float32
        )
        grad_value = jnp.einsum(
            "hgqk,qhgd->khd",
            probs.astype(jnp.bfloat16),
            grad_out,
            preferred_element_type=jnp.float32,
        )
        return (
            grad_query,
            (grad_key.reshape(block, width_kv), grad_value.reshape(block, width_kv)),
        )

    start_query = jnp.zeros((rows_here, KV_HEADS, group, HEAD_DIM), jnp.float32)
    grad_query, (grad_keys, grad_values) = lax.scan(grad_step, start_query, items)
    return (
        grad_query,
        grad_keys.reshape(count * block, width_kv),
        grad_values.reshape(count * block, width_kv),
    )


def local(tokens, attention_weights, feedforward_weights, norm_gains, span_order, cotangent):
    ctx_count = lax.axis_size("ctx")
    batch_count = lax.axis_size("batch")
    rows_here = tokens.shape[1]
    halves = rows_here // 2
    length = rows_here * ctx_count
    group = HEADS // KV_HEADS
    width_q = HEADS * HEAD_DIM
    width_kv = KV_HEADS * HEAD_DIM
    block = math.gcd(length, 512)
    scaling = HEAD_DIM ** (-0.5)
    att_full, ff_full = (
        lax.all_gather(attention_weights, ("batch", "ctx"), axis=0, tiled=True),
        lax.all_gather(feedforward_weights, ("batch", "ctx"), axis=0, tiled=True),
    )
    gain_full = lax.all_gather(norm_gains, "ctx", axis=1, tiled=True)
    order_full = lax.all_gather(span_order, "ctx", axis=1, tiled=True)
    offsets = jnp.arange(halves, dtype=jnp.int32)
    key_pos = (order_full[0][:, None] * halves + offsets[None, :]).reshape(length)
    query_pos = (span_order[0][:, None] * halves + offsets[None, :]).reshape(rows_here)
    cos_table, sin_table = rope_tables(query_pos)
    (w_query, w_key, w_value, w_out), (w_gate, w_up, w_down) = unpack(att_full, ff_full)
    inputs = tokens[0].astype(jnp.float32)
    hidden_f, norm_one_pull = jax.vjp(normalize, inputs, gain_full[0])
    hidden = hidden_f.astype(jnp.bfloat16)
    query_raw = jnp.dot(hidden, w_query, preferred_element_type=jnp.float32).reshape(
        rows_here, HEADS, HEAD_DIM
    )
    key_raw = jnp.dot(hidden, w_key, preferred_element_type=jnp.float32).reshape(
        rows_here, KV_HEADS, HEAD_DIM
    )
    values = jnp.dot(hidden, w_value, preferred_element_type=jnp.float32).astype(jnp.bfloat16)
    query_rot, query_pull = jax.vjp(lambda a: rotate(a, cos_table, sin_table), query_raw)
    key_rot, key_pull = jax.vjp(lambda a: rotate(a, cos_table, sin_table), key_raw)
    queries = query_rot.astype(jnp.bfloat16).reshape(rows_here, KV_HEADS, group, HEAD_DIM)
    keys = key_rot.astype(jnp.bfloat16).reshape(rows_here, width_kv)
    key_all, value_all = (
        lax.all_gather(keys, "ctx", axis=0, tiled=True),
        lax.all_gather(values, "ctx", axis=0, tiled=True),
    )
    attended, log_total = attention_forward(queries, key_all, value_all, query_pos, key_pos, block)
    attended_low = attended.reshape(rows_here, width_q).astype(jnp.bfloat16)
    middle = inputs + jnp.dot(attended_low, w_out, preferred_element_type=jnp.float32)
    hidden_two_f, norm_two_pull = jax.vjp(normalize, middle, gain_full[1])
    hidden_two = hidden_two_f.astype(jnp.bfloat16)
    gate = jnp.dot(hidden_two, w_gate, preferred_element_type=jnp.float32)
    upward = jnp.dot(hidden_two, w_up, preferred_element_type=jnp.float32)
    activ_f, swiglu_pull = jax.vjp(swiglu, gate, upward)
    activ = activ_f.astype(jnp.bfloat16)
    result = middle + jnp.dot(activ, w_down, preferred_element_type=jnp.float32)
    att_back, ff_back = (
        lax.all_gather(attention_weights, ("batch", "ctx"), axis=0, tiled=True),
        lax.all_gather(feedforward_weights, ("batch", "ctx"), axis=0, tiled=True),
    )
    (w_query, w_key, w_value, w_out), (w_gate, w_up, w_down) = unpack(att_back, ff_back)
    key_all, value_all = (
        lax.all_gather(keys, "ctx", axis=0, tiled=True),
        lax.all_gather(values, "ctx", axis=0, tiled=True),
    )
    grad_result = cotangent[0]
    grad_down = jnp.einsum("tf,td->fd", activ, grad_result, preferred_element_type=jnp.float32)
    grad_activ = jnp.einsum("td,fd->tf", grad_result, w_down, preferred_element_type=jnp.float32)
    grad_gate_f, grad_up_f = swiglu_pull(grad_activ)
    grad_gate = grad_gate_f.astype(jnp.bfloat16)
    grad_upward = grad_up_f.astype(jnp.bfloat16)
    grad_w_gate = jnp.einsum("td,tf->df", hidden_two, grad_gate, preferred_element_type=jnp.float32)
    grad_w_up = jnp.einsum("td,tf->df", hidden_two, grad_upward, preferred_element_type=jnp.float32)
    grad_hidden_two = jnp.einsum("tf,df->td", grad_gate, w_gate, preferred_element_type=jnp.float32)
    grad_hidden_two = grad_hidden_two + jnp.einsum(
        "tf,df->td", grad_upward, w_up, preferred_element_type=jnp.float32
    )
    grad_middle_norm, grad_gain_two = norm_two_pull(grad_hidden_two)
    grad_middle = grad_result.astype(jnp.float32) + grad_middle_norm
    grad_branch = grad_middle.astype(jnp.bfloat16)
    grad_w_out = jnp.einsum(
        "tq,td->qd", attended_low, grad_branch, preferred_element_type=jnp.float32
    )
    grad_attended = jnp.einsum(
        "td,qd->tq", grad_branch, w_out, preferred_element_type=jnp.float32
    ).astype(jnp.bfloat16)
    grad_attended = grad_attended.reshape(rows_here, KV_HEADS, group, HEAD_DIM)
    grad_query_rot, grad_key_all, grad_value_all = attention_backward(
        queries, key_all, value_all, query_pos, key_pos, block, log_total, grad_attended, attended
    )
    grad_key_rot, grad_value_f = (
        lax.psum_scatter(
            grad_key_all.astype(jnp.bfloat16), "ctx", scatter_dimension=0, tiled=True
        ).astype(jnp.float32),
        lax.psum_scatter(
            grad_value_all.astype(jnp.bfloat16), "ctx", scatter_dimension=0, tiled=True
        ).astype(jnp.float32),
    )
    grad_query_raw = query_pull(grad_query_rot.reshape(rows_here, HEADS, HEAD_DIM) * scaling)[0]
    grad_key_raw = key_pull(grad_key_rot.reshape(rows_here, KV_HEADS, HEAD_DIM) * scaling)[0]
    grad_query = grad_query_raw.reshape(rows_here, width_q).astype(jnp.bfloat16)
    grad_key = grad_key_raw.reshape(rows_here, width_kv).astype(jnp.bfloat16)
    grad_value = grad_value_f.astype(jnp.bfloat16)
    grad_w_query = jnp.einsum("td,tq->dq", hidden, grad_query, preferred_element_type=jnp.float32)
    grad_w_key = jnp.einsum("td,tq->dq", hidden, grad_key, preferred_element_type=jnp.float32)
    grad_w_value = jnp.einsum("td,tq->dq", hidden, grad_value, preferred_element_type=jnp.float32)
    grad_hidden = jnp.einsum("tq,dq->td", grad_query, w_query, preferred_element_type=jnp.float32)
    grad_hidden = grad_hidden + jnp.einsum(
        "tq,dq->td", grad_key, w_key, preferred_element_type=jnp.float32
    )
    grad_hidden = grad_hidden + jnp.einsum(
        "tq,dq->td", grad_value, w_value, preferred_element_type=jnp.float32
    )
    grad_inputs_norm, grad_gain_one = norm_one_pull(grad_hidden)
    grad_inputs = grad_middle + grad_inputs_norm
    grad_att_flat = jnp.concatenate(
        [
            grad_w_query.reshape(-1),
            grad_w_key.reshape(-1),
            grad_w_value.reshape(-1),
            grad_w_out.reshape(-1),
        ]
    )
    grad_ff_flat = jnp.concatenate(
        [grad_w_gate.reshape(-1), grad_w_up.reshape(-1), grad_down.reshape(-1)]
    )
    width_own = D // ctx_count
    gain_terms = jnp.stack([grad_gain_one, grad_gain_two]).reshape(2, ctx_count, width_own)
    gain_terms = jnp.transpose(gain_terms, (1, 0, 2)).reshape(ctx_count, 2 * width_own)
    gain_terms = jnp.broadcast_to(
        gain_terms[None], (batch_count, ctx_count, 2 * width_own)
    ).reshape(batch_count * ctx_count, 2 * width_own)
    att_part, ff_part, gain_part = (
        lax.psum_scatter(
            grad_att_flat.astype(jnp.bfloat16), "batch", scatter_dimension=0, tiled=True
        ).astype(jnp.float32),
        lax.psum_scatter(
            grad_ff_flat.astype(jnp.bfloat16), "batch", scatter_dimension=0, tiled=True
        ).astype(jnp.float32),
        lax.psum_scatter(
            gain_terms.astype(jnp.bfloat16), "batch", scatter_dimension=0, tiled=True
        ).astype(jnp.float32),
    )
    grad_att_own, grad_ff_own, gain_own = (
        lax.psum_scatter(
            att_part.astype(jnp.bfloat16), "ctx", scatter_dimension=0, tiled=True
        ).astype(jnp.float32),
        lax.psum_scatter(
            ff_part.astype(jnp.bfloat16), "ctx", scatter_dimension=0, tiled=True
        ).astype(jnp.float32),
        lax.psum_scatter(
            gain_part.astype(jnp.bfloat16), "ctx", scatter_dimension=0, tiled=True
        ).astype(jnp.float32),
    )
    grad_gain_own = gain_own.reshape(2, width_own)
    return (
        result.astype(jnp.bfloat16)[None],
        grad_inputs[None],
        grad_att_own,
        grad_ff_own,
        grad_gain_own,
    )


def solution(mesh):
    placed = (
        P("batch", "ctx", None),
        P(("batch", "ctx")),
        P(("batch", "ctx")),
        P(None, "ctx"),
        P("batch", "ctx"),
        P("batch", "ctx", None),
    )
    return jax.shard_map(
        local,
        mesh=mesh,
        in_specs=placed,
        out_specs=(
            P("batch", "ctx", None),
            P("batch", "ctx", None),
            P(("batch", "ctx")),
            P(("batch", "ctx")),
            P(None, "ctx"),
        ),
        check_vma=False,
    )
```

profile of v0, /device:TPU:0, one launch (start us, length us, event | category | flops | bytes accessed | tf_op | source)
XLA Modules:
  0.0 884.2 jit_solution(17290509841535917515)
XLA Ops:
  12.2 10.6 %all-reduce.4 = s32[16]{0:T(128)S(1)} all-reduce(s32[16]{0:T(128)S(1)} %bitcast_dynamic-update-slice_fusion), channel_id=1, replica_groups=mesh['batch'=4,'ctx'=8] {'ctx'}, use_global_device_ids=true, to_apply=%add.4 | all-reduce | flops 16 | bytes 128
  24.8 9.5 %all-gather = f32[8,120,2]{1,2,0:T(2,128)S(1)} all-gather(f32[1,120,2]{1,2,0:T(2,128)} %bitcast.319), channel_id=1, replica_groups=mesh['batch'=4,'ctx'=8] {'ctx'}, dimensions={0}, use_global_device_ids=true | all-gather | bytes 8640 | tf_op jit(solution)/shard_map/all_gather | solution.py:175
  34.7 43.4 %all-gather.4.cloned.1.call-done = bf16[2457600]{0:T(1024)(128)(2,1)} async-done(((bf16[76800]{0:T(1024)(128)(2,1)}), bf16[2457600]{0:T(1024)(128)(2,1)}) %all-gather.4.cloned.1.call-update) | async-done | bytes 4915216 | tf_op jit(solution)/shard_map/all_gather | solution.py:172
  90.7 23.2 %all_gather.25 = bf16[1536,320]{1,0:T(8,128)(2,1)} all-gather(bf16[192,320]{1,0:T(8,128)(2,1)S(1)} %copy.48), channel_id=1, replica_groups=mesh['batch'=4,'ctx'=8] {'ctx'}, dimensions={0}, use_global_device_ids=true | all-gather | bytes 1105920 | tf_op jit(solution)/shard_map/all_gather | solution.py:197
  117.1 25.7 %all_gather.26 = bf16[1536,320]{1,0:T(8,128)(2,1)} all-gather(bf16[192,320]{1,0:T(8,128)(2,1)S(1)} %convolution_convert_fusion.8), channel_id=1, replica_groups=mesh['batch'=4,'ctx'=8] {'ctx'}, dimensions={0}, use_global_device_ids=true | all-gather | bytes 1105920 | tf_op jit(solution)/shard_map/all_gather | solution.py:198
  145.1 4.3 slice.122
  149.5 3.8 copy.49
  156.3 22.0 %while.30 = (s32[]{:T(128)}, f32[5,3,192]{2,1,0:T(4,128)S(1)}, f32[5,3,192]{2,1,0:T(4,128)S(1)}, f32[192,5,3,64]{0,3,2,1:T(8,128)}, s32[3,512]{1,0:T(4,128)S(1)}...) while((s32[]{:T(128)}, f32[5,3,192]{2,1,0:T(4,128)S(1)}, ...), condition=%wide.region_4.5_spmd.clone, body=%wide.region_1.4_spmd.clone.sunk | while | flops 397325376 | bytes 27989192 | solution.py:102
  183.1 17.0 %all-gather.6.cloned.1.call-done = bf16[7372800]{0:T(1024)(128)(2,1)} async-done(((bf16[230400]{0:T(1024)(128)(2,1)}), bf16[7372800]{0:T(1024)(128)(2,1)}) %all-gather.6.cloned.1.call-update) | async-done | bytes 14745616 | tf_op jit(solution)/shard_map/all_gather | solution.py:173
  200.1 11.2 %fusion.74 = (bf16[2457600]{0:T(1024)(128)(2,1)}, bf16[2457600]{0:T(1024)(128)(2,1)}, bf16[2457600]{0:T(1024)(128)(2,1)}) fusion(bf16[7372800]{0:T(1024)(128)(2,1)} %all-gather.6.cloned.1.call-done), kind=kLoop, calls=%fused_computation.144 | loop fusion | bytes 29491200 | tf_op jit(solution)/shard_map/slice | solution.py:50
  211.3 9.5 %slice.135 = bf16[2560,960]{1,0:T(8,128)(2,1)} reshape(bf16[2457600]{0:T(1024)(128)(2,1)} %get-tuple-element.341) | data formatting | bytes 9830400 | tf_op jit(solution)/shard_map/slice | solution.py:50
  220.8 10.0 %slice.133 = bf16[960,2560]{1,0:T(8,128)(2,1)} reshape(bf16[2457600]{0:T(1024)(128)(2,1)} %get-tuple-element.342) | data formatting | bytes 9830400 | tf_op jit(solution)/shard_map/slice | solution.py:50
  230.8 10.5 %slice.131 = bf16[960,2560]{1,0:T(8,128)(2,1)} reshape(bf16[2457600]{0:T(1024)(128)(2,1)} %get-tuple-element.343) | data formatting | bytes 9830400 | tf_op jit(solution)/shard_map/slice | solution.py:50
  241.3 3.7 fusion.82
  246.9 3.6 multiply_convert_fusion
  260.3 26.8 %while.31 = (s32[]{:T(128)}, f32[192,5,3,64]{0,3,2,1:T(8,128)S(1)}, bf16[3,512,320]{1,2,0:T(8,128)(2,1)}, bf16[3,512,320]{1,2,0:T(8,128)(2,1)}, bf16[3,512,320]{...) while((s32[]{:T(128)}, f32[192,5,3,64]{0,3,2,1:T(8,128)S(1)}, ...), condition=%wide.region_9.10_spmd.clone, body=%wide.region_8.9_spmd.clone.sunk | while | flops 958931136 | bytes 35564488 | solution.py:152
  292.1 3.7 convolution_convert_fusion
  295.9 7.9 copy.60
  303.8 10.6 %reshape.462 = bf16[2457600]{0:T(1024)(128)(2,1)} reshape(bf16[2560,960]{1,0:T(8,128)(2,1)} %copy.60) | data formatting | bytes 9830400 | tf_op jit(solution)/shard_map/reshape | solution.py:278
  314.4 3.7 convolution_convert_fusion.1
  318.1 10.3 %reshape.461 = bf16[2457600]{0:T(1024)(128)(2,1)} reshape(bf16[960,2560]{1,0:T(8,128)(2,1)} %convolution_convert_fusion.1) | data formatting | bytes 9830400 | tf_op jit(solution)/shard_map/reshape | solution.py:278
  328.4 3.7 convolution_convert_fusion.2
  332.1 10.2 %reshape.460 = bf16[2457600]{0:T(1024)(128)(2,1)} reshape(bf16[960,2560]{1,0:T(8,128)(2,1)} %convolution_convert_fusion.2) | data formatting | bytes 9830400 | tf_op jit(solution)/shard_map/reshape | solution.py:278
  342.5 18.5 %pad_maximum_fusion = bf16[7372800]{0:T(1024)(128)(2,1)} fusion(bf16[2457600]{0:T(1024)(128)(2,1)} %reshape.462, bf16[2457600]{0:T(1024)(128)(2,1)} %reshape.461, bf16[2457600]{0:T(1024)(128)(2,1)} %reshape.460), kind=kLoop, calls=%fused_computation.45 | loop fusion | flops 44236800 | bytes 29491200 | tf_op jit(solution)/shard_map/concatenate | solution.py:277
  362.9 4.8 reshape.459
  388.5 15.0 %pad_maximum_fusion.1 = bf16[2457600]{0:T(1024)(128)(2,1)} fusion(bf16[921600]{0:T(1024)(128)(2,1)S(1)} %copy-done.9, bf16[307200]{0:T(1024)(128)(2,1)} %reshape.458, bf16[307200]{0:T(1024)(128)(2,1)} %reshape.457, bf16[921600]{0:T(1024)(128)(2,1)} %reshape.456), kind=kLoop, calls=%fused_computation.49 | loop fusion | flops 19660800 | bytes 9830400 | tf_op jit(solution)/shard_map/concatenate | solution.py:269
  406.1 350.4 %all-reduce.18.cloned.1.call-done = (bf16[2457600]{0:T(1024)(128)(2,1)}, bf16[7372800]{0:T(1024)(128)(2,1)}) async-done(((bf16[2457600]{0:T(1024)(128)(2,1)}, bf16[7372800]{0:T(1024)(128)(2,1)}), (bf16[2457600]{0:T(1024)(128)(2,1)}, bf16[7372800]{0:T(1024)(128)(2,1)})) %all-reduce.18.cloned.1.call-update) | async-done | bytes 19660816
  758.9 3.5 dynamic-slice.6
  765.4 5.4 fusion.37
  772.2 14.8 %all-reduce.9 = bf16[32,240]{1,0:T(8,128)(2,1)S(1)} all-reduce(bf16[32,240]{1,0:T(8,128)(2,1)S(1)} %broadcast_bitcast_fusion), channel_id=8, replica_groups=mesh['batch'=4,'ctx'=8] {'batch'}, use_global_device_ids=true, to_apply=%region_19.20.clone | all-reduce | flops 7680 | bytes 30720
  787.0 14.6 %all-reduce.10 = bf16[8,240]{1,0:T(8,128)(2,1)S(1)} all-reduce(bf16[8,240]{1,0:T(8,128)(2,1)S(1)} %constant_dynamic-slice_fusion.6), channel_id=9, replica_groups=mesh['batch'=4,'ctx'=8] {'ctx'}, use_global_device_ids=true, to_apply=%region_20.21.clone | all-reduce | flops 1920 | bytes 7680
  804.1 69.3 %all-reduce.16.cloned.1.call-done = (bf16[614400]{0:T(1024)(128)(2,1)}, bf16[1843200]{0:T(1024)(128)(2,1)}) async-done(((bf16[614400]{0:T(1024)(128)(2,1)}, bf16[1843200]{0:T(1024)(128)(2,1)}), (bf16[614400]{0:T(1024)(128)(2,1)}, bf16[1843200]{0:T(1024)(128)(2,1)})) %all-reduce.16.cloned.1.call-update) | async-done | bytes 4915216
  (266 shorter events, 132.1 us)
Async XLA Ops:
  7.2 70.9 %all-gather.4.cloned.1.call-start = ((), (), s32[]{:S(2)}) async-start(), calls=%async_computation.2 | async-start | bytes 5068800 | tf_op jit(solution)/shard_map/all_gather | solution.py:172
  7.9 192.2 %all-gather.6.cloned.1.call-start = ((), (), s32[]{:S(2)}) async-start(), calls=%async_computation.3 | async-start | bytes 15206400 | tf_op jit(solution)/shard_map/all_gather | solution.py:173
  8.6 363.5 %reduce-scatter.5.cloned.1.call-start = ((), (), s32[]{:S(2)}) async-start(), calls=%async_computation.5 | async-start | bytes 1327104 | tf_op jit(solution)/shard_map/reduce_scatter | solution.py:248
  24.0 129.2 %copy-start.32 = (f32[192]{0:T(256)}, f32[192]{0:T(256)S(1)}, u32[]{:S(2)}) copy-start(f32[192]{0:T(256)S(1)} %fusion.68) | copy-start | bytes 2308
  34.4 118.9 %copy-start.30 = (f32[1,960]{1,0:T(1,128)}, f32[1,960]{1,0:T(1,128)S(1)}, u32[]{:S(2)}) copy-start(f32[1,960]{1,0:T(1,128)S(1)} %get-tuple-element.360) | copy-start | bytes 11524
  34.6 121.4 %copy-start.25 = (f32[192,32]{0,1:T(8,128)}, f32[192,32]{0,1:T(8,128)S(1)}, u32[]{:S(2)}) copy-start(f32[192,32]{0,1:T(8,128)S(1)} %get-tuple-element.361) | copy-start | bytes 73732
  34.7 121.4 %copy-start.27 = (f32[192,32]{0,1:T(8,128)}, f32[192,32]{0,1:T(8,128)S(1)}, u32[]{:S(2)}) copy-start(f32[192,32]{0,1:T(8,128)S(1)} %get-tuple-element.362) | copy-start | bytes 73732
  85.2 4.8 copy-start.3
  89.7 53.1 %copy-start.10 = (bf16[960,320]{1,0:T(8,128)(2,1)}, bf16[960,320]{1,0:T(8,128)(2,1)S(1)}, u32[]{:S(2)}) copy-start(bf16[960,320]{1,0:T(8,128)(2,1)S(1)} %slice.118) | copy-start | bytes 1843204
  241.3 5.1 slice-start.2
  245.1 7.0 slice-start
  246.9 5.2 slice-start.1
  287.1 5.0 copy-start.17
  287.1 5.0 copy-start.20
  289.6 89.9 %reduce-scatter.3.cloned.1.call-start = ((), (), s32[]{:S(2)}) async-start(), calls=%async_computation.4 | async-start | bytes 1327104 | tf_op jit(solution)/shard_map/reduce_scatter | solution.py:245
  303.8 10.6 %copy-start.24 = (bf16[192,2560]{1,0:T(8,128)(2,1)S(1)}, bf16[192,2560]{1,0:T(8,128)(2,1)}, u32[]{:S(2)}) copy-start(bf16[192,2560]{1,0:T(8,128)(2,1)} %copy-done.23) | copy-start | bytes 2949124
  318.1 10.3 %copy-start.22 = (bf16[192,2560]{1,0:T(8,128)(2,1)S(1)}, bf16[192,2560]{1,0:T(8,128)(2,1)}, u32[]{:S(2)}) copy-start(bf16[192,2560]{1,0:T(8,128)(2,1)} %copy-done.21) | copy-start | bytes 2949124
  342.4 18.5 %copy-start.5 = (f32[192,960]{1,0:T(8,128)S(1)}, f32[192,960]{1,0:T(8,128)}, u32[]{:S(2)}) copy-start(f32[192,960]{1,0:T(8,128)} %copy-done.4) | copy-start | bytes 2211844
  342.4 18.5 %copy-start.13 = (bf16[192,5,3,64]{0,3,2,1:T(8,128)(2,1)S(1)}, bf16[192,5,3,64]{0,3,2,1:T(8,128)(2,1)}, u32[]{:S(2)}) copy-start(bf16[192,5,3,64]{0,3,2,1:T(8,128)(2,1)} %copy-done.12) | copy-start | bytes 1105924
  342.4 414.1 %all-reduce.18.cloned.1.call-start = ((), (), s32[]{:S(2)}) async-start(), calls=%async_computation.7 | async-start | bytes 39321600
  360.9 6.8 copy-start.26
  360.9 6.8 copy-start.28
  362.9 5.1 copy-start.31
  362.9 5.1 copy-start.33
  372.2 16.4 %copy-start.9 = (bf16[921600]{0:T(1024)(128)(2,1)S(1)}, bf16[921600]{0:T(1024)(128)(2,1)}, u32[]{:S(2)}) copy-start(bf16[921600]{0:T(1024)(128)(2,1)} %reshape.459) | copy-start | bytes 5529604
  403.6 469.8 %all-reduce.16.cloned.1.call-start = ((), (), s32[]{:S(2)}) async-start(), calls=%async_computation.6 | async-start | bytes 9830400
  758.9 5.7 copy-start.1
  764.6 6.3 copy-start.11
  765.4 5.9 copy-start.16
  765.4 5.9 copy-start.29
  765.4 37.6 %copy-start.35 = (f32[192]{0:T(256)S(1)}, f32[192]{0:T(256)}, u32[]{:S(2)}) copy-start(f32[192]{0:T(256)} %copy-done.34) | copy-start | bytes 2308
  765.4 37.6 %copy-start.6 = (f32[192,960]{1,0:T(8,128)S(1)}, f32[192,960]{1,0:T(8,128)}, u32[]{:S(2)}) copy-start(f32[192,960]{1,0:T(8,128)} %copy-done.4) | copy-start | bytes 2211844
  (21 other events, 43.5 us)
Sparse Core Ops, SparseCore 0:
  10.8 67.1 all-gather.3
  80.9 119.1 all-gather.5
  289.7 31.0 reduce-scatter.4
  342.5 30.8 reduce-scatter.2
  403.7 352.7 all-reduce.17
  762.6 110.7 all-reduce.15
where the time goes:
time: 891 us; the launch traced here: 884 us
  waiting for transfers between devices  482 us (54%)
  local copies, waits for them, and re-layouts  156 us (18%)
  blocking collectives  98.6 us (11%)
  matrix products  74.6 us (8%)
  other arithmetic  53.7 us (6%)
  between operations  19 us (2%)
    unnamed x8, waiting for transfers between devices  421 us
    slice x10, local copies, waits for them, and re-layouts, split_flat(): flat[offset:offset + rows_in * cols_in].reshape(rows_in, cols_in)  57.2 us
    all_gather x1, waiting for transfers between devices, local(): lax.all_gather(attention_weights, ('batch', 'ctx'), axis=0, tiled=True)  43.4 us
    unnamed x3, blocking collectives  40.1 us
    all_gather x1, blocking collectives, local(): lax.all_gather(values, 'ctx', axis=0, tiled=True)  25.7 us
    all_gather x1, blocking collectives, local(): lax.all_gather(keys, 'ctx', axis=0, tiled=True)  23.2 us
    concatenate x1, other arithmetic, local(): jnp.concatenate([grad_w_gate.reshape(-1), grad_w_up.reshape(-1), grad_dow...  18.5 us
  transfers between devices with their start and end apart: 6, of which 4 were waited for; matrix products, arithmetic and copies ran while one was open for 18% of the time, Pallas kernels for 0%

commit v1 on v0

--- a/solution.py
+++ b/solution.py
@@ -3,6 +3,8 @@
 import jax
 import jax.numpy as jnp
 from jax import lax
+from jax.experimental import pallas as pl
+from jax.experimental.pallas import tpu as pltpu
 from jax.sharding import PartitionSpec as P
 
 D = 960
@@ -157,7 +159,7 @@
     )
 
 
-def local(tokens, attention_weights, feedforward_weights, norm_gains, span_order, cotangent):
+def local_any(tokens, attention_weights, feedforward_weights, norm_gains, span_order, cotangent):
     ctx_count = lax.axis_size("ctx")
     batch_count = lax.axis_size("batch")
     rows_here = tokens.shape[1]
@@ -207,15 +209,6 @@
     activ_f, swiglu_pull = jax.vjp(swiglu, gate, upward)
     activ = activ_f.astype(jnp.bfloat16)
     result = middle + jnp.dot(activ, w_down, preferred_element_type=jnp.float32)
-    att_back, ff_back = (
-        lax.all_gather(attention_weights, ("batch", "ctx"), axis=0, tiled=True),
-        lax.all_gather(feedforward_weights, ("batch", "ctx"), axis=0, tiled=True),
-    )
-    (w_query, w_key, w_value, w_out), (w_gate, w_up, w_down) = unpack(att_back, ff_back)
-    key_all, value_all = (
-        lax.all_gather(keys, "ctx", axis=0, tiled=True),
-        lax.all_gather(values, "ctx", axis=0, tiled=True),
-    )
     grad_result = cotangent[0]
     grad_down = jnp.einsum("tf,td->fd", activ, grad_result, preferred_element_type=jnp.float32)
     grad_activ = jnp.einsum("td,fd->tf", grad_result, w_down, preferred_element_type=jnp.float32)
@@ -315,7 +308,627 @@
     )
 
 
+CHUNK = 4
+
+
+def sort_rows(spans_ref, own_ref, other_ref, sorted_ref, span):
+    for m, ref in enumerate((own_ref, other_ref)):
+        for z in range(4):
+            for j in range(2):
+                start = pl.multiple_of(spans_ref[m, z, j] * span, span)
+                sorted_ref[pl.ds(start, span), :] = ref[z, j * span : (j + 1) * span, :]
+
+
+def group_rows(ref, part, span, head):
+    group = HEADS // KV_HEADS
+    rows = ref[part * span : (part + 1) * span, :]
+    columns = [
+        rows[:, (head * group + j) * HEAD_DIM : (head * group + j + 1) * HEAD_DIM]
+        for j in range(group)
+    ]
+    return jnp.concatenate(columns, 0)
+
+
+def seen(position, step, span, rows, cols):
+    row = lax.broadcasted_iota(jnp.int32, (rows, cols), 0) % span
+    col = lax.broadcasted_iota(jnp.int32, (rows, cols), 1)
+    return col + step * cols <= row + position * span
+
+
+def attend_kernel(
+    spans_ref, q_ref, own_ref, other_ref, out_ref, lse_ref, sorted_ref, q_scr, top_ref, sum_ref, acc_ref
+):
+    group = HEADS // KV_HEADS
+    span = q_ref.shape[0] // 2
+    width_kv = KV_HEADS * HEAD_DIM
+    rows, cols = group * span, CHUNK * span
+    sort_rows(spans_ref, own_ref, other_ref, sorted_ref, span)
+    for part in range(2):
+        position = spans_ref[0, 4, part]
+        for g in range(KV_HEADS):
+            q_scr[g] = group_rows(q_ref, part, span, g) * jnp.bfloat16(HEAD_DIM**-0.5)
+        top_ref[...] = jnp.full(top_ref.shape, NEG, jnp.float32)
+        sum_ref[...] = jnp.zeros(sum_ref.shape, jnp.float32)
+        acc_ref[...] = jnp.zeros(acc_ref.shape, jnp.float32)
+
+        def step(i, unused):
+            visible = seen(position, i, span, rows, cols)
+            base = pl.multiple_of(i * cols, cols)
+            for g in range(KV_HEADS):
+                k = sorted_ref[pl.ds(base, cols), g * HEAD_DIM : (g + 1) * HEAD_DIM]
+                v = sorted_ref[
+                    pl.ds(base, cols), width_kv + g * HEAD_DIM : width_kv + (g + 1) * HEAD_DIM
+                ]
+                s = lax.dot_general(
+                    q_scr[g], k, (((1,), (1,)), ((), ())), preferred_element_type=jnp.float32
+                )
+                s = jnp.where(visible, s, NEG)
+                old = top_ref[g]
+                top = jnp.maximum(old, jnp.max(s, 1, keepdims=True))
+                weights = jnp.where(visible, jnp.exp(s - top), 0.0)
+                factor = jnp.exp(old - top)
+                top_ref[g] = top
+                sum_ref[g] = sum_ref[g] * factor + jnp.sum(weights, 1, keepdims=True)
+                acc_ref[g] = acc_ref[g] * factor + jnp.dot(
+                    weights.astype(jnp.bfloat16), v, preferred_element_type=jnp.float32
+                )
+            return 0
+
+        lax.fori_loop(0, (position + CHUNK) // CHUNK, step, 0)
+        for g in range(KV_HEADS):
+            out = acc_ref[g] / sum_ref[g]
+            lse_ref[part * KV_HEADS + g] = top_ref[g] + jnp.log(sum_ref[g])
+            for j in range(group):
+                h = g * group + j
+                out_ref[part * span : (part + 1) * span, h * HEAD_DIM : (h + 1) * HEAD_DIM] = out[
+                    j * span : (j + 1) * span
+                ]
+
+
+def attend(spans, queries, own, other):
+    rows, width = queries.shape
+    group = HEADS // KV_HEADS
+    stacked = group * rows // 2
+    vmem = pl.BlockSpec(memory_space=pltpu.VMEM)
+    return pl.pallas_call(
+        attend_kernel,
+        out_shape=(
+            jax.ShapeDtypeStruct((rows, width), jnp.float32),
+            jax.ShapeDtypeStruct((2 * KV_HEADS, stacked, 1), jnp.float32),
+        ),
+        in_specs=[pl.BlockSpec(memory_space=pltpu.SMEM), vmem, vmem, vmem],
+        out_specs=(vmem, vmem),
+        scratch_shapes=[
+            pltpu.VMEM((8 * rows, own.shape[2]), jnp.bfloat16),
+            pltpu.VMEM((KV_HEADS, stacked, HEAD_DIM), jnp.bfloat16),
+            pltpu.VMEM((KV_HEADS, stacked, 1), jnp.float32),
+            pltpu.VMEM((KV_HEADS, stacked, 1), jnp.float32),
+            pltpu.VMEM((KV_HEADS, stacked, HEAD_DIM), jnp.float32),
+        ],
+        compiler_params=pltpu.CompilerParams(vmem_limit_bytes=24 * 2**20),
+        name="attend",
+    )(spans, queries, own, other)
+
+
+def attend_back_kernel(
+    spans_ref, q_ref, own_ref, other_ref, out_ref, lse_ref, grad_ref,
+    dq_ref, own_grad_ref, other_grad_ref,
+    sorted_ref, q_scr, grad_scr, delta_ref, dq_scr, dk_scr, dv_scr,
+):
+    group = HEADS // KV_HEADS
+    span = q_ref.shape[0] // 2
+    width_kv = KV_HEADS * HEAD_DIM
+    rows, cols = group * span, CHUNK * span
+    sort_rows(spans_ref, own_ref, other_ref, sorted_ref, span)
+    dk_scr[...] = jnp.zeros(dk_scr.shape, jnp.float32)
+    dv_scr[...] = jnp.zeros(dv_scr.shape, jnp.float32)
+    for part in range(2):
+        position = spans_ref[0, 4, part]
+        for g in range(KV_HEADS):
+            q_scr[g] = group_rows(q_ref, part, span, g) * jnp.bfloat16(HEAD_DIM**-0.5)
+            grad = group_rows(grad_ref, part, span, g)
+            grad_scr[g] = grad
+            delta_ref[g] = jnp.sum(
+                grad.astype(jnp.float32) * group_rows(out_ref, part, span, g), 1, keepdims=True
+            )
+        dq_scr[...] = jnp.zeros(dq_scr.shape, jnp.float32)
+
+        def step(i, unused):
+            visible = seen(position, i, span, rows, cols)
+            base = pl.multiple_of(i * cols, cols)
+            for g in range(KV_HEADS):
+                k = sorted_ref[pl.ds(base, cols), g * HEAD_DIM : (g + 1) * HEAD_DIM]
+                v = sorted_ref[
+                    pl.ds(base, cols), width_kv + g * HEAD_DIM : width_kv + (g + 1) * HEAD_DIM
+                ]
+                q, grad = q_scr[g], grad_scr[g]
+                s = lax.dot_general(
+                    q, k, (((1,), (1,)), ((), ())), preferred_element_type=jnp.float32
+                )
+                probs = jnp.where(visible, jnp.exp(s - lse_ref[part * KV_HEADS + g]), 0.0)
+                grad_probs = lax.dot_general(
+                    grad, v, (((1,), (1,)), ((), ())), preferred_element_type=jnp.float32
+                )
+                grad_s = (probs * (grad_probs - delta_ref[g])).astype(jnp.bfloat16)
+                dq_scr[g] += jnp.dot(grad_s, k, preferred_element_type=jnp.float32)
+                dk_scr[g, pl.ds(base, cols), :] += lax.dot_general(
+                    grad_s, q, (((0,), (0,)), ((), ())), preferred_element_type=jnp.float32
+                )
+                dv_scr[g, pl.ds(base, cols), :] += lax.dot_general(
+                    probs.astype(jnp.bfloat16), grad, (((0,), (0,)), ((), ())),
+                    preferred_element_type=jnp.float32,
+                )
+            return 0
+
+        lax.fori_loop(0, (position + CHUNK) // CHUNK, step, 0)
+        for g in range(KV_HEADS):
+            dq = dq_scr[g] * HEAD_DIM**-0.5
+            for j in range(group):
+                h = g * group + j
+                dq_ref[part * span : (part + 1) * span, h * HEAD_DIM : (h + 1) * HEAD_DIM] = dq[
+                    j * span : (j + 1) * span
+                ]
+    for m, ref in enumerate((own_grad_ref, other_grad_ref)):
+        for z in range(4):
+            for j in range(2):
+                start = pl.multiple_of(spans_ref[m, z, j] * span, span)
+                parts = [scr[g, pl.ds(start, span), :] for scr in (dk_scr, dv_scr) for g in range(KV_HEADS)]
+                ref[z, j * span : (j + 1) * span, :] = jnp.concatenate(parts, 1).astype(jnp.bfloat16)
+
+
+def attend_back(spans, queries, own, other, out, lse, grad):
+    rows, width = queries.shape
+    group = HEADS // KV_HEADS
+    stacked = group * rows // 2
+    wide = own.shape[2]
+    vmem = pl.BlockSpec(memory_space=pltpu.VMEM)
+    return pl.pallas_call(
+        attend_back_kernel,
+        out_shape=(
+            jax.ShapeDtypeStruct((rows, width), jnp.float32),
+            jax.ShapeDtypeStruct((4, rows, wide), jnp.bfloat16),
+            jax.ShapeDtypeStruct((4, rows, wide), jnp.bfloat16),
+        ),
+        in_specs=[pl.BlockSpec(memory_space=pltpu.SMEM)] + [vmem] * 6,
+        out_specs=(vmem, vmem, vmem),
+        scratch_shapes=[
+            pltpu.VMEM((8 * rows, wide), jnp.bfloat16),
+            pltpu.VMEM((KV_HEADS, stacked, HEAD_DIM), jnp.bfloat16),
+            pltpu.VMEM((KV_HEADS, stacked, HEAD_DIM), jnp.bfloat16),
+            pltpu.VMEM((KV_HEADS, stacked, 1), jnp.float32),
+            pltpu.VMEM((KV_HEADS, stacked, HEAD_DIM), jnp.float32),
+            pltpu.VMEM((KV_HEADS, 8 * rows, HEAD_DIM), jnp.float32),
+            pltpu.VMEM((KV_HEADS, 8 * rows, HEAD_DIM), jnp.float32),
+        ],
+        compiler_params=pltpu.CompilerParams(vmem_limit_bytes=32 * 2**20),
+        name="attend_back",
+    )(spans, queries, own, other, out, lse, grad)
+
+
+BF = jnp.bfloat16
+F32 = jnp.float32
+LANES = 128
+GU_PAD = 96
+X_PAIRS = [(j, j ^ 1) for j in range(4)]
+Y_PAIRS = [(j, j ^ 2) for j in range(4)]
+CORE_PAIRS = [(j, j ^ 1) for j in range(8)]
+EXTRA = 2
+
+
+def up_pairs(first, last):
+    return [(2 * z + c, 2 * z + 2 + c) for z in range(first, last) for c in range(2)]
+
+
+def down_pairs(first, last):
+    return [(2 * z + 2 + c, 2 * z + c) for z in range(first, last) for c in range(2)]
+
+
+def swap_x(a):
+    return lax.ppermute(a, "batch", X_PAIRS)
+
+
+def swap_y(a):
+    return lax.ppermute(a, "batch", Y_PAIRS)
+
+
+def swap_core(a):
+    return lax.ppermute(a, "ctx", CORE_PAIRS)
+
+
+def tiles(a):
+    rows, cols = a.shape
+    a = a.reshape(rows // 8, 8, cols // LANES, LANES)
+    return a.transpose(0, 2, 1, 3).reshape(rows * cols // (8 * LANES), 8, LANES)
+
+
+def untile(a, cols):
+    rows = a.shape[0] * 8 * LANES // cols
+    a = a.reshape(rows // 8, cols // LANES, 8, LANES)
+    return a.transpose(0, 2, 1, 3).reshape(rows, cols)
+
+
+def pad_to(a, rows, cols):
+    return jnp.pad(a, ((0, rows - a.shape[0]), (0, cols - a.shape[1])))
+
+
+def halves_of(a):
+    half = a.shape[1] // 2
+    return jnp.stack([tiles(a[:, :half]), tiles(a[:, half:])])
+
+
+def whole_of(pair, cols):
+    return jnp.concatenate([untile(pair[0], cols // 2), untile(pair[1], cols // 2)], 1)
+
+
+def gather_line(a, z):
+    u1 = lax.ppermute(a, "ctx", up_pairs(0, 3))
+    d1 = lax.ppermute(a, "ctx", down_pairs(0, 3))
+    u2 = lax.ppermute(u1, "ctx", up_pairs(1, 3))
+    d2 = lax.ppermute(d1, "ctx", down_pairs(0, 2))
+    u3 = lax.ppermute(u2, "ctx", up_pairs(2, 3))
+    d3 = lax.ppermute(d2, "ctx", down_pairs(0, 1))
+    seven = jnp.stack([u3, u2, u1, a, d1, d2, d3])
+    return lax.dynamic_slice_in_dim(seven, 3 - z, 4, 0)
+
+
+def gather_plane(a):
+    first, second = a[:2], a[2:]
+    x_first = swap_x(first)
+    y_second = swap_y(second)
+    x_second = swap_x(second)
+    y_first = swap_y(first)
+    diag_first = swap_y(x_first)
+    diag_second = swap_x(y_second)
+    return ((first, second), (x_first, x_second), (y_first, y_second), (diag_first, diag_second))
+
+
+def place(pieces, b, start, stop):
+    shape = pieces[0][0].shape
+    whole = jnp.zeros((4, 4, shape[1], stop - start, 8, LANES), BF)
+    for step, pair in enumerate(pieces):
+        for part, piece in enumerate(pair):
+            whole = lax.dynamic_update_slice(
+                whole, piece[None, :, :, start:stop], (b ^ step, 2 * part, 0, 0, 0, 0)
+            )
+    return whole
+
+
+def add(*terms):
+    total = terms[0].astype(F32)
+    for term in terms[1:]:
+        total = total + term.astype(F32)
+    return total.astype(BF)
+
+
+def scatter_plane(g, b):
+    own, xs, ys, ds = [lax.dynamic_index_in_dim(g, b ^ k, 0, keepdims=False) for k in range(4)]
+    diag_first = swap_x(ds[:2])
+    diag_second = swap_y(ds[2:])
+    x_first = swap_x(xs[:2])
+    y_second = swap_y(ys[2:])
+    x_second = swap_x(add(xs[2:], diag_second))
+    y_first = swap_y(add(ys[:2], diag_first))
+    return jnp.concatenate(
+        [add(own[:2], x_first, y_first), add(own[2:], x_second, y_second)], 0
+    )
+
+
+def scatter_line(t, z):
+    def block(k):
+        return lax.dynamic_index_in_dim(t, jnp.clip(z + k, 0, 3), 0, keepdims=False)
+
+    def pass_on(a, first, last, way):
+        if way > 0:
+            got = lax.ppermute(a, "ctx", up_pairs(first, last))
+            return jnp.where((z > first) & (z <= last), got, 0)
+        got = lax.ppermute(a, "ctx", down_pairs(first, last))
+        return jnp.where((z >= first) & (z < last), got, 0)
+
+    up = pass_on(block(3), 0, 1, 1)
+    down = pass_on(block(-3), 2, 3, -1)
+    up = pass_on(add(block(2), up), 0, 2, 1)
+    down = pass_on(add(block(-2), down), 1, 3, -1)
+    up = pass_on(add(block(1), up), 0, 3, 1)
+    down = pass_on(add(block(-1), down), 0, 3, -1)
+    return block(0).astype(F32) + up.astype(F32) + down.astype(F32)
+
+
+def split_high(a, parts):
+    out = []
+    for unused in range(parts):
+        high = lax.reduce_precision(a, 8, 7)
+        out.append(high.astype(BF))
+        a = a - high
+    return out
+
+
+def local_block(tokens, attention_weights, feedforward_weights, norm_gains, span_order, cotangent):
+    rows_here = tokens.shape[1]
+    halves = rows_here // 2
+    width_q = HEADS * HEAD_DIM
+    width_kv = KV_HEADS * HEAD_DIM
+    wide = 2 * 512
+    b = lax.axis_index("batch")
+    place_ctx = lax.axis_index("ctx")
+    z = place_ctx // 2
+    c = place_ctx % 2
+    device = b * 8 + place_ctx
+    own_gain = D // 8
+
+    def pick(first, second):
+        return jnp.where(c == 0, first, second)
+
+    def merge(mine, other):
+        return pick(
+            jnp.concatenate([mine, other], -1), jnp.concatenate([other, mine], -1)
+        )
+
+    def half_of(a, k):
+        half = a.shape[-1] // 2
+        return jnp.where((c ^ k) == 0, a[..., :half], a[..., half:])
+
+    def pair_up(shard):
+        mine = pick(shard[0], shard[1])
+        other = swap_core(pick(shard[1], shard[0]))
+        return pick(jnp.stack([mine, other]), jnp.stack([other, mine]))
+
+    att_rows = attention_weights.shape[0] // D
+    att_shard = halves_of(pad_to(attention_weights.reshape(att_rows, D), att_rows, wide))
+    gain_parts = jnp.stack(split_high(norm_gains, 3), 1)
+    gain_rows = jnp.pad(gain_parts, ((0, 0), (0, 8 * EXTRA - 3), (0, LANES - own_gain)))
+    gain_rows = gain_rows.reshape(2, EXTRA, 8, LANES)
+    att_chip = pair_up(jnp.concatenate([att_shard, gain_rows], 1))
+    att_pieces = gather_plane(gather_line(att_chip, z))
+    att_body = att_rows * wide // (2 * 8 * LANES)
+    att_mine = place(att_pieces, b, 0, att_body).reshape(-1, 8, LANES)
+    gain_mine = place(att_pieces, b, att_body, att_body + EXTRA)
+    att_other = swap_core(att_mine)
+    gain_other = swap_core(gain_mine)
+
+    def gain_from(a):
+        parts = a[0, :, :, 0, :3, :own_gain].astype(F32)
+        return (parts[:, :, 0] + parts[:, :, 1] + parts[:, :, 2]).reshape(D)
+
+    gain_m, gain_o = gain_from(gain_mine), gain_from(gain_other)
+    gain_full = jnp.stack([pick(gain_m, gain_o), pick(gain_o, gain_m)])
+
+    gu_rows = feedforward_weights.shape[0] // FF
+    down_rows = feedforward_weights.shape[0] // D
+    mixed = 2 * D // gu_rows
+    rest = 2 * D - mixed * gu_rows
+    rest_pad = -(-rest // 8) * 8
+    gu_shard = halves_of(pad_to(feedforward_weights.reshape(gu_rows, FF), GU_PAD, FF))
+    down_shard = halves_of(pad_to(feedforward_weights.reshape(down_rows, D), down_rows, wide))
+    mixed_shard = jnp.concatenate(
+        [
+            halves_of(pad_to(feedforward_weights[: rest * FF].reshape(rest, FF), rest_pad, FF)),
+            halves_of(
+                pad_to(feedforward_weights[rest * FF :].reshape(-1, D), down_rows - rest * FF // D, wide)
+            ),
+        ],
+        1,
+    )
+    ff_shard = jnp.where(device < mixed, gu_shard, jnp.where(device == mixed, mixed_shard, down_shard))
+    ff_pieces = gather_plane(gather_line(pair_up(ff_shard), z))
+    ff_body = ff_shard.shape[1]
+    ff_mine = place(ff_pieces, b, 0, ff_body).reshape(-1, 8, LANES)
+    ff_other = swap_core(ff_mine)
+    gu_total = mixed * GU_PAD + rest_pad
+    gu_cut = gu_total * FF // (2 * 8 * LANES)
+
+    def matrices(a):
+        return untile(a[:gu_cut], FF // 2), untile(a[gu_cut:], wide // 2)
+
+    gu_m, down_m = matrices(ff_mine)
+    gu_o, down_o = matrices(ff_other)
+
+    pad_row = jnp.arange(gu_total, dtype=jnp.int32)
+    true_row = pad_row // GU_PAD * gu_rows + pad_row % GU_PAD
+    real = pad_row % GU_PAD < gu_rows
+    is_gate = real & (true_row < D)
+    is_up = real & (true_row >= D)
+    spread = ((true_row % D)[None, :] == jnp.arange(D, dtype=jnp.int32)[:, None]) & real[None, :]
+    spread = spread.astype(BF)
+    third = D // 3
+    order3 = jnp.arange(D, dtype=jnp.int32)
+    perm3 = (order3[:, None] == (order3 % third * 3 + order3 // third)[None, :]).astype(BF)
+
+    offsets = jnp.arange(halves, dtype=jnp.int32)
+    query_pos = (span_order[0][:, None] * halves + offsets[None, :]).reshape(rows_here)
+    cos_table, sin_table = rope_tables(query_pos)
+
+    inputs = tokens[0].astype(F32)
+    hidden_f, norm_one_pull = jax.vjp(normalize, inputs, gain_full[0])
+    hidden = hidden_f.astype(BF)
+    hidden3 = jnp.dot(hidden, perm3, preferred_element_type=F32).astype(BF)
+    hidden3 = hidden3.reshape(rows_here, 3, third)
+    att_m, att_o = untile(att_mine, wide // 2), untile(att_other, wide // 2)
+    cut_k, cut_v, cut_o = D, D + third, D + 2 * third
+
+    def project(a, start, stop):
+        return merge(
+            jnp.dot(a, att_m[start:stop], preferred_element_type=F32),
+            jnp.dot(a, att_o[start:stop], preferred_element_type=F32),
+        )
+
+    def thirds(start, stop):
+        out = project(hidden3.transpose(1, 0, 2).reshape(3 * rows_here, third), start, stop)
+        out = out.reshape(3, rows_here, wide)
+        return out[0, :, :third] + out[1, :, third : 2 * third] + out[2, :, 2 * third : 3 * third]
+
+    query_raw = project(hidden, 0, D)[:, :width_q].reshape(rows_here, HEADS, HEAD_DIM)
+    key_raw = thirds(cut_k, cut_v).reshape(rows_here, KV_HEADS, HEAD_DIM)
+    values = thirds(cut_v, cut_o).astype(BF)
+    query_rot, query_pull = jax.vjp(lambda a: rotate(a, cos_table, sin_table), query_raw)
+    key_rot, key_pull = jax.vjp(lambda a: rotate(a, cos_table, sin_table), key_raw)
+    queries = query_rot.astype(BF).reshape(rows_here, width_q)
+    keys = key_rot.astype(BF).reshape(rows_here, width_kv)
+
+    span_rows = jnp.pad(span_order.astype(BF), ((0, 15), (0, 2 * width_kv - 2)))
+    key_value = jnp.concatenate([jnp.concatenate([keys, values], 1), span_rows], 0)
+    line_mine = gather_line(key_value, z)
+    line_other = swap_core(line_mine)
+    spans = jnp.stack([line_mine[:, rows_here, :2], line_other[:, rows_here, :2]]).astype(jnp.int32)
+    spans = jnp.concatenate([spans, jnp.broadcast_to(span_order[None], (2, 1, 2))], 1)
+    attended, log_total = attend(spans, queries, line_mine, line_other)
+    attended_low = attended.astype(BF)
+    middle = inputs + project(attended_low, cut_o, cut_o + D)[:, :D]
+    hidden_two_f, norm_two_pull = jax.vjp(normalize, middle, gain_full[1])
+    hidden_two = hidden_two_f.astype(BF)
+    spread_two = jnp.dot(hidden_two, spread, preferred_element_type=F32).astype(BF)
+    for_gate = jnp.where(is_gate[None, :], spread_two, 0)
+    for_up = jnp.where(is_up[None, :], spread_two, 0)
+    gate_end = -(-D // gu_rows) * GU_PAD
+    up_start = D // gu_rows * GU_PAD
+
+    def widen(a, start, stop):
+        return merge(
+            jnp.dot(a[:, start:stop], gu_m[start:stop], preferred_element_type=F32),
+            jnp.dot(a[:, start:stop], gu_o[start:stop], preferred_element_type=F32),
+        )
+
+    gate = widen(for_gate, 0, gate_end)
+    upward = widen(for_up, up_start, gu_total)
+    activ_f, swiglu_pull = jax.vjp(swiglu, gate, upward)
+    activ = activ_f.astype(BF)
+    result = middle + merge(
+        jnp.dot(activ, down_m, preferred_element_type=F32),
+        jnp.dot(activ, down_o, preferred_element_type=F32),
+    )[:, :D]
+
+    grad_result = cotangent[0]
+    grad_wide = jnp.pad(grad_result, ((0, 0), (0, wide - D)))
+
+    def times_transposed(a, w):
+        return lax.dot_general(a, w, (((1,), (1,)), ((), ())), preferred_element_type=F32)
+
+    def transposed_times(a, w):
+        return lax.dot_general(a, w, (((0,), (0,)), ((), ())), preferred_element_type=F32)
+
+    grad_activ = times_transposed(half_of(grad_wide, 0), down_m)
+    grad_activ = grad_activ + times_transposed(half_of(grad_wide, 1), down_o)
+    grad_gate_f, grad_up_f = swiglu_pull(grad_activ)
+    grad_gate = grad_gate_f.astype(BF)
+    grad_upward = grad_up_f.astype(BF)
+    stacked_in = jnp.concatenate([for_gate, for_up], 0)
+    stacked_out = jnp.concatenate([grad_gate, grad_upward], 0)
+
+    def ff_terms(k):
+        gu = transposed_times(stacked_in, half_of(stacked_out, k)).astype(BF)
+        down = transposed_times(activ, half_of(grad_wide, k)).astype(BF)
+        return jnp.concatenate([tiles(gu), tiles(down)], 0)
+
+    ff_from = swap_core(ff_terms(1))
+    ff_sum = add(ff_terms(0), ff_from).reshape(4, 4, 2, ff_body, 8, LANES)
+    ff_own = scatter_line(scatter_plane(ff_sum, b), z)
+
+    def narrow(a, start, stop):
+        return times_transposed(half_of(a, 0), gu_m[start:stop]) + times_transposed(
+            half_of(a, 1), gu_o[start:stop]
+        )
+
+    back_gate = jnp.where(is_gate[None, :gate_end], narrow(grad_gate, 0, gate_end), 0.0)
+    back_up = jnp.where(is_up[None, up_start:], narrow(grad_upward, up_start, gu_total), 0.0)
+
+    def collapse(a, start, stop):
+        parts = jnp.concatenate(split_high(a, 2), 1)
+        table = jnp.concatenate([spread[:, start:stop]] * 2, 1)
+        return times_transposed(parts, table)
+
+    grad_hidden_two = collapse(back_gate, 0, gate_end) + collapse(back_up, up_start, gu_total)
+    grad_middle_norm, grad_gain_two = norm_two_pull(grad_hidden_two)
+    grad_middle = grad_result.astype(F32) + grad_middle_norm
+    grad_branch = grad_middle.astype(BF)
+    branch_wide = jnp.pad(grad_branch, ((0, 0), (0, wide - D)))
+
+    def project_back(a, start, stop):
+        return times_transposed(half_of(a, 0), att_m[start:stop]) + times_transposed(
+            half_of(a, 1), att_o[start:stop]
+        )
+
+    grad_attended = project_back(branch_wide, cut_o, cut_o + D).astype(BF)
+    grad_query_rot, both_mine, both_other = attend_back(
+        spans, queries, line_mine, line_other, attended, log_total, grad_attended
+    )
+    both_from = swap_core(both_other.astype(BF))
+    both_own = scatter_line(add(both_mine, both_from), z)
+    grad_key_rot, grad_value_f = both_own[:, :width_kv], both_own[:, width_kv:]
+    grad_query_raw = query_pull(grad_query_rot.reshape(rows_here, HEADS, HEAD_DIM))[0]
+    grad_key_raw = key_pull(grad_key_rot.reshape(rows_here, KV_HEADS, HEAD_DIM))[0]
+    grad_query = grad_query_raw.reshape(rows_here, width_q).astype(BF)
+    grad_key = grad_key_raw.reshape(rows_here, width_kv).astype(BF)
+    grad_value = grad_value_f.astype(BF)
+
+    def spots(a):
+        return jnp.concatenate(
+            [jnp.pad(a, ((0, 0), (q * third, wide - (q + 1) * third))) for q in range(3)], 0
+        )
+
+    query_wide = jnp.pad(grad_query, ((0, 0), (0, wide - D)))
+    key_spots, value_spots = spots(grad_key), spots(grad_value)
+    hidden_rows = hidden3.transpose(1, 0, 2).reshape(3 * rows_here, third)
+    back_three = project_back(key_spots, cut_k, cut_v) + project_back(value_spots, cut_v, cut_o)
+    back_three = back_three.reshape(3, rows_here, third).transpose(1, 0, 2).reshape(rows_here, D)
+    grad_hidden = project_back(query_wide, 0, D) + times_transposed(
+        jnp.concatenate(split_high(back_three, 2), 1), jnp.concatenate([perm3, perm3], 1)
+    )
+    grad_inputs_norm, grad_gain_one = norm_one_pull(grad_hidden)
+    grad_inputs = grad_middle + grad_inputs_norm
+
+    gain_terms = jnp.stack([grad_gain_one, grad_gain_two]).reshape(2, 8, own_gain)
+    gain_terms = jnp.pad(
+        jnp.stack(split_high(gain_terms, 2), 2),
+        ((0, 0), (0, 0), (0, 8 * EXTRA - 2), (0, LANES - own_gain)),
+    ).reshape(2, 4, 2, EXTRA, 8, LANES)
+
+    def att_terms(k):
+        terms = jnp.concatenate(
+            [
+                transposed_times(hidden, half_of(query_wide, k)).astype(BF),
+                transposed_times(hidden_rows, half_of(key_spots, k)).astype(BF),
+                transposed_times(hidden_rows, half_of(value_spots, k)).astype(BF),
+                transposed_times(attended_low, half_of(branch_wide, k)).astype(BF),
+            ],
+            0,
+        )
+        gain = jnp.where((c ^ k) == 0, gain_terms[0], gain_terms[1])
+        gain = jnp.broadcast_to(gain[None], (4, 4, 2, EXTRA, 8, LANES))
+        return jnp.concatenate([tiles(terms).reshape(4, 4, 2, att_body, 8, LANES), gain], 3)
+
+    att_from = swap_core(att_terms(1))
+    att_own = scatter_line(scatter_plane(add(att_terms(0), att_from), b), z)
+
+    def settle(own):
+        mine = pick(own[0], own[1])
+        other = swap_core(pick(own[1], own[0]))
+        return pick(jnp.stack([mine, other]), jnp.stack([other, mine]))
+
+    ff_done = settle(ff_own)
+    att_done = settle(att_own)
+    gain_own = att_done[:, att_body, 0, :own_gain] + att_done[:, att_body, 1, :own_gain]
+    att_flat = whole_of(att_done[:, :att_body], wide)[:, :D].reshape(-1)
+    gu_flat = whole_of(ff_done, FF)[:gu_rows].reshape(-1)
+    down_flat = whole_of(ff_done, wide)[:, :D].reshape(-1)
+    cut = rest_pad * FF // (2 * 8 * LANES)
+    mixed_flat = jnp.concatenate(
+        [
+            whole_of(ff_done[:, :cut], FF)[:rest].reshape(-1),
+            whole_of(ff_done[:, cut:], wide)[:, :D].reshape(-1),
+        ]
+    )
+    ff_flat = jnp.where(device < mixed, gu_flat, jnp.where(device == mixed, mixed_flat, down_flat))
+    return (
+        result.astype(BF)[None],
+        grad_inputs[None],
+        att_flat,
+        ff_flat,
+        gain_own,
+    )
+
+
 def solution(mesh):
+    fits = mesh.shape["batch"] == 4 and mesh.shape["ctx"] == 8
+    local = local_block if fits else local_any
     placed = (
         P("batch", "ctx", None),
         P(("batch", "ctx")),

time: 891 us -> 548 us (0.62)
  waiting for transfers between devices: 482 us -> 190 us
  starting transfers between devices: 0.24 us -> 103 us
  blocking collectives: 98.6 us -> 0 us
  local copies, waits for them, and re-layouts: 156 us -> 71.8 us
  Pallas kernels: 0 us -> 30.8 us
  other arithmetic: 53.7 us -> 69.8 us
  between operations: 19 us -> 3.18 us
    unnamed x8 -> x0, waiting for transfers between devices: 421 us -> none
    ppermute x0 -> x71, waiting for transfers between devices: none -> 190 us  [the longest x12 64.9 us: swap_x(): return lax.ppermute(a, 'batch', X_PAIRS)]
    ppermute x0 -> x71, starting transfers between devices: none -> 103 us  [the longest x9 36.8 us: pass_on(): got = lax.ppermute(a, 'ctx', up_pairs(first, last))]
    all_gather x2 -> x0, waiting for transfers between devices: 60.4 us -> none  [the longest x1 43.4 us: local(): lax.all_gather(attention_weights, ('batch', 'ctx'), axis=0, tiled=True)]
    all_gather x3 -> x0, blocking collectives: 58.5 us -> none  [the longest x1 25.7 us: local(): lax.all_gather(values, 'ctx', axis=0, tiled=True)]
    reshape x8 -> x10, local copies, waits for them, and re-layouts: 45.4 us -> 4.82 us  [the longest x1 1.09 us: local_block(): attention_weights.reshape(att_rows, D)]
    unnamed x3 -> x0, blocking collectives: 40.1 us -> none
    convert_element_type x7 -> x29, other arithmetic: 5.17 us -> 43.7 us  [the longest x16 34.7 us: add(): return total.astype(BF)]
  transfers between devices with their start and end apart: 6 -> 71, of which waited for: 4 -> 32; matrix products, arithmetic and copies ran while one was open for 18% -> 31% of each run, Pallas kernels for 0% -> 3%
where the time goes in v1:
time: 548 us; the launch traced here: 541 us
  waiting for transfers between devices  190 us (35%)
  starting transfers between devices  103 us (19%)
  matrix products  72.9 us (13%)
  local copies, waits for them, and re-layouts  71.8 us (13%)
  other arithmetic  69.8 us (13%)
  Pallas kernels  30.8 us (6%)
    ppermute x12, waiting for transfers between devices, swap_x(): return lax.ppermute(a, 'batch', X_PAIRS)  64.9 us
    ppermute x12, waiting for transfers between devices, swap_y(): return lax.ppermute(a, 'batch', Y_PAIRS)  56.6 us
    ppermute x9, starting transfers between devices, pass_on(): got = lax.ppermute(a, 'ctx', up_pairs(first, last))  36.8 us
    convert_element_type x16, other arithmetic, add(): return total.astype(BF)  34.7 us
    dot_general x17, matrix products, times_transposed(): lax.dot_general(a, w, (((1,), (1,)), ((), ())), preferred_element_type=F32)  31 us
    ppermute x9, waiting for transfers between devices, pass_on(): got = lax.ppermute(a, 'ctx', up_pairs(first, last))  23.8 us
    dot_general x12, matrix products, transposed_times(): lax.dot_general(a, w, (((0,), (0,)), ((), ())), preferred_element_type=F32)  21 us
    ppermute x3, waiting for transfers between devices, gather_line(): d3 = lax.ppermute(d2, 'ctx', down_pairs(0, 1))  19.8 us
  transfers between devices with their start and end apart: 71, of which 32 were waited for; matrix products, arithmetic and copies ran while one was open for 31% of the time, Pallas kernels for 3%

profile of v1, /device:TPU:0, one launch (start us, length us, event | category | flops | bytes accessed | tf_op | source)
XLA Modules:
  0.0 541.1 jit_solution(6434031244662283784)
XLA Ops:
  5.9 4.7 collective-permute-start.1
  24.5 5.8 %collective-permute-start.23 = (bf16[2,120,8,128]{3,2,1,0:T(8,128)(2,1)S(1)}, bf16[2,120,8,128]{3,2,1,0:T(8,128)(2,1)S(1)}, u32[]{:S(2)}, u32[]{:S(2)}) collective-permute-start(bf16[2,120,8,128]{3,2,1,0:T(8,128)(2,1)S(1)} %maximum_select_fusion.8), channel_id=1, source_target_pairs={{0,2},{1,3},{2,4},{3,5},{4,6},{5,7},{8,10},{9,11},{10,12},{11,13},... | collective-permute-start | bytes 1474568 | tf_op jit(solution)/shard_map/ppermute | solution.py:564
  35.4 6.4 %collective-permute-done.6 = bf16[2,42,8,128]{3,2,1,0:T(8,128)(2,1)S(1)} collective-permute-done((bf16[2,42,8,128]{3,2,1,0:T(8,128)(2,1)}, bf16[2,42,8,128]{3,2,1,0:T(8,128)(2,1)S(1)}, u32[]{:S(2)}, u32[]{:S(2)}) %collective-permute-start.6) | collective-permute-done | bytes 172064 | tf_op jit(solution)/shard_map/ppermute | solution.py:569
  51.0 7.5 %collective-permute-done.7 = bf16[2,2,42,8,128]{4,3,2,1,0:T(8,128)(2,1)S(1)} collective-permute-done((bf16[2,2,42,8,128]{4,3,2,1,0:T(8,128)(2,1)S(1)}, bf16[2,2,42,8,128]{4,3,2,1,0:T(8,128)(2,1)S(1)}, u32[]{:S(2)}, u32[]{:S(2)}) %collective-permute-start.7) | collective-permute-done | bytes 344096 | tf_op jit(solution)/shard_map/ppermute | solution.py:527
  70.4 5.1 collective-permute-done.28
  75.6 4.9 broadcast_in_dim.219
  92.0 16.5 %collective-permute-done.32 = bf16[2,2,120,8,128]{4,3,2,1,0:T(8,128)(2,1)S(1)} collective-permute-done((bf16[2,2,120,8,128]{4,3,2,1,0:T(8,128)(2,1)}, bf16[2,2,120,8,128]{4,3,2,1,0:T(8,128)(2,1)S(1)}, u32[]{:S(2)}, u32[]{:S(2)}) %collective-permute-start.32) | collective-permute-done | bytes 983072 | tf_op jit(solution)/shard_map/ppermute | solution.py:531
  112.9 18.4 %collective-permute-done.30 = bf16[2,2,120,8,128]{4,3,2,1,0:T(8,128)(2,1)} collective-permute-done((bf16[2,2,120,8,128]{4,3,2,1,0:T(8,128)(2,1)}, bf16[2,2,120,8,128]{4,3,2,1,0:T(8,128)(2,1)}, u32[]{:S(2)}, u32[]{:S(2)}) %collective-permute-start.30) | collective-permute-done | bytes 983072 | tf_op jit(solution)/shard_map/ppermute | solution.py:527
  135.5 9.2 %collective-permute-done.33 = bf16[2,2,120,8,128]{4,3,2,1,0:T(8,128)(2,1)S(1)} collective-permute-done((bf16[2,2,120,8,128]{4,3,2,1,0:T(8,128)(2,1)}, bf16[2,2,120,8,128]{4,3,2,1,0:T(8,128)(2,1)S(1)}, u32[]{:S(2)}, u32[]{:S(2)}) %collective-permute-start.33) | collective-permute-done | bytes 983072 | tf_op jit(solution)/shard_map/ppermute | solution.py:531
  161.2 4.0 slice.803
  170.1 6.9 %collective-permute-done.18 = bf16[208,640]{1,0:T(8,128)(2,1)S(1)} collective-permute-done((bf16[208,640]{1,0:T(8,128)(2,1)S(1)}, bf16[208,640]{1,0:T(8,128)(2,1)S(1)}, u32[]{:S(2)}, u32[]{:S(2)}) %collective-permute-start.18) | collective-permute-done | bytes 266272 | tf_op jit(solution)/shard_map/ppermute | solution.py:565
  182.7 6.8 %slice.786 = bf16[2560,8,128]{2,1,0:T(8,128)(2,1)} slice(bf16[3840,8,128]{2,1,0:T(8,128)(2,1)} %bitcast.121), slice={[0:2560], [0:8], [0:128]} | slice | bytes 10485760 | tf_op jit(solution)/shard_map/slice | solution.py:720
  191.1 8.3 %collective-permute-done.20 = bf16[208,640]{1,0:T(8,128)(2,1)S(1)} collective-permute-done((bf16[208,640]{1,0:T(8,128)(2,1)S(1)}, bf16[208,640]{1,0:T(8,128)(2,1)S(1)}, u32[]{:S(2)}, u32[]{:S(2)}) %collective-permute-start.20) | collective-permute-done | bytes 266272 | tf_op jit(solution)/shard_map/ppermute | solution.py:569
  208.8 13.7 %attend.1 = (f32[192,960]{1,0:T(8,128)S(1)}, f32[10,288,1]{2,1,0:T(8,128)S(1)}) custom-call(s32[2,5,2]{2,1,0:T(8,128)S(1)} %copy.163.spans_ref, bf16[192,960]{1,0:T(8,128)(2,1)S(1)} %copy.164.q_ref, bf16[4,208,640]{2,1,0:T(8,128)(2,1)S(1)} %constant_dynamic-slice_fusion.7.own_ref, bf16[4,208,640]{2,1,0:T(8,128)(2,1)S(1)} %collective-permute-done.21.other_ref), custom_call_target="tpu_custom_call" | custom-call | tf_op jit(solution)/shard_map/attend/pallas_call | solution.py:393
  244.6 4.8 convolution_convert_fusion
  261.7 17.2 %attend_back.1 = (f32[192,960]{1,0:T(8,128)S(1)}, bf16[4,192,640]{2,1,0:T(8,128)(2,1)S(1)}, bf16[4,192,640]{2,1,0:T(8,128)(2,1)S(1)}) custom-call(s32[2,5,2]{2,1,0:T(8,128)S(1)} %copy.163.spans_ref, bf16[192,960]{1,0:T(8,128)(2,1)S(1)} %copy.164.q_ref, bf16[4,208,640]{2,1,0:T(8,128)(2,1)S(1)} %constant_dynamic-slice_fusion.7.own_ref, ...), custom_call_target="tpu_custom_call" | custom-call | tf_op jit(solution)/shard_map/attend_back/pallas_call | solution.py:485
  286.7 9.1 %pad_maximum_fusion = bf16[3840,8,128]{2,1,0:T(8,128)(2,1)} fusion(bf16[1280,8,128]{2,1,0:T(8,128)(2,1)} %bitcast.612, bf16[2560,8,128]{2,1,0:T(8,128)(2,1)} %bitcast.623), kind=kLoop, calls=%fused_computation.1 | loop fusion | flops 3932160 | bytes 15728640 | tf_op jit(solution)/shard_map/concatenate | solution.py:819
  307.5 4.4 collective-permute-start.38
  319.4 5.0 collective-permute-start.39
  328.7 5.9 %collective-permute-done.42 = bf16[192,640]{1,0:T(8,128)(2,1)S(1)} collective-permute-done((bf16[192,640]{1,0:T(8,128)(2,1)S(1)}, bf16[192,640]{1,0:T(8,128)(2,1)S(1)}, u32[]{:S(2)}, u32[]{:S(2)}) %collective-permute-start.42) | collective-permute-done | bytes 245792 | tf_op jit(solution)/shard_map/ppermute | solution.py:624
  360.8 28.9 %add_convert_fusion = bf16[3840,8,128]{2,1,0:T(8,128)(2,1)S(1)} fusion(bf16[3840,8,128]{2,1,0:T(8,128)(2,1)} %collective-permute-done.57, bf16[1280,8,128]{2,1,0:T(8,128)(2,1)S(1)} %bitcast.611, bf16[2560,8,128]{2,1,0:T(8,128)(2,1)S(1)} %bitcast.624), kind=kLoop, calls=%fused_computation | loop fusion | flops 19660800 | bytes 23592960 | tf_op jit(solution)/shard_map/convert_element_type | solution.py:600
  396.2 18.6 %collective-permute-done.61 = bf16[2,2,120,8,128]{4,3,2,1,0:T(8,128)(2,1)S(1)} collective-permute-done((bf16[2,2,120,8,128]{4,3,2,1,0:T(8,128)(2,1)S(1)}, bf16[2,2,120,8,128]{4,3,2,1,0:T(8,128)(2,1)S(1)}, u32[]{:S(2)}, u32[]{:S(2)}) %collective-permute-start.61) | collective-permute-done | bytes 983072 | tf_op jit(solution)/shard_map/ppermute | solution.py:531
  417.2 5.0 collective-permute-done.47
  423.0 21.8 %collective-permute-done.45 = bf16[2,2,42,8,128]{4,3,2,1,0:T(8,128)(2,1)S(1)} collective-permute-done((bf16[2,2,42,8,128]{4,3,2,1,0:T(8,128)(2,1)S(1)}, bf16[2,2,42,8,128]{4,3,2,1,0:T(8,128)(2,1)S(1)}, u32[]{:S(2)}, u32[]{:S(2)}) %collective-permute-start.45) | collective-permute-done | bytes 344096 | tf_op jit(solution)/shard_map/ppermute | solution.py:527
  450.2 4.7 collective-permute-done.48
  471.2 9.6 %collective-permute-done.58 = bf16[2,2,120,8,128]{4,3,2,1,0:T(8,128)(2,1)S(1)} collective-permute-done((bf16[2,2,120,8,128]{4,3,2,1,0:T(8,128)(2,1)S(1)}, bf16[2,2,120,8,128]{4,3,2,1,0:T(8,128)(2,1)S(1)}, u32[]{:S(2)}, u32[]{:S(2)}) %collective-permute-start.58) | collective-permute-done | bytes 983072 | tf_op jit(solution)/shard_map/ppermute | solution.py:527
  488.4 8.8 %collective-permute-done.51 = bf16[2,42,8,128]{3,2,1,0:T(8,128)(2,1)S(1)} collective-permute-done((bf16[2,42,8,128]{3,2,1,0:T(8,128)(2,1)S(1)}, bf16[2,42,8,128]{3,2,1,0:T(8,128)(2,1)S(1)}, u32[]{:S(2)}, u32[]{:S(2)}) %collective-permute-start.51) | collective-permute-done | bytes 172064 | tf_op jit(solution)/shard_map/ppermute | solution.py:622
  497.4 4.4 collective-permute-start.52
  503.7 4.6 collective-permute-start.65
  510.6 4.6 collective-permute-done.65
  515.8 7.7 %collective-permute-start.66 = (bf16[2,120,8,128]{3,2,1,0:T(8,128)(2,1)S(1)}, bf16[2,120,8,128]{3,2,1,0:T(8,128)(2,1)S(1)}, u32[]{:S(2)}, u32[]{:S(2)}) collective-permute-start(bf16[2,120,8,128]{3,2,1,0:T(8,128)(2,1)S(1)} %get-tuple-element.41), channel_id=1, source_target_pairs={{0,2},{1,3},{2,4},{3,5},{4,6},{5,7},{8,10},{9,11},{10,12},{11,13},... | collective-permute-start | bytes 1474568 | tf_op jit(solution)/shard_map/ppermute | solution.py:622
  529.8 4.4 collective-permute-done.69
  (493 shorter events, 250.4 us)
Async XLA Ops:
  4.9 18.2 %collective-permute-start.22 = (bf16[120,8,128]{2,1,0:T(8,128)(2,1)S(1)}, bf16[120,8,128]{2,1,0:T(8,128)(2,1)S(1)}, u32[]{:S(2)}, u32[]{:S(2)}) collective-permute-start(bf16[120,8,128]{2,1,0:T(8,128)(2,1)S(1)} %get-tuple-element.84), channel_id=1, source_target_pairs={{0,1},{1,0},{2,3},{3,2},{4,5},{5,4},{6,7},{7,6},{8,9},{9,8},{10,11... | collective-permute-start | bytes 737288 | tf_op jit(solution)/shard_map/ppermute | solution.py:535
  23.2 26.0 %collective-permute-start.26 = (bf16[2,120,8,128]{3,2,1,0:T(8,128)(2,1)S(1)}, bf16[2,120,8,128]{3,2,1,0:T(8,128)(2,1)S(1)}, u32[]{:S(2)}, u32[]{:S(2)}) collective-permute-start(bf16[2,120,8,128]{3,2,1,0:T(8,128)(2,1)S(1)} %maximum_select_fusion.8), channel_id=1, source_target_pairs={{2,0},{3,1},{4,2},{5,3},{6,4},{7,5},{10,8},{11,9},{12,10},{13,11},... | collective-permute-start | bytes 1474568 | tf_op jit(solution)/shard_map/ppermute | solution.py:565
  24.5 25.3 %collective-permute-start.23 = (bf16[2,120,8,128]{3,2,1,0:T(8,128)(2,1)S(1)}, bf16[2,120,8,128]{3,2,1,0:T(8,128)(2,1)S(1)}, u32[]{:S(2)}, u32[]{:S(2)}) collective-permute-start(bf16[2,120,8,128]{3,2,1,0:T(8,128)(2,1)S(1)} %maximum_select_fusion.8), channel_id=1, source_target_pairs={{0,2},{1,3},{2,4},{3,5},{4,6},{5,7},{8,10},{9,11},{10,12},{11,13},... | collective-permute-start | bytes 1474568 | tf_op jit(solution)/shard_map/ppermute | solution.py:564
  42.0 18.0 %collective-permute-start.10 = (bf16[2,2,42,8,128]{4,3,2,1,0:T(8,128)(2,1)S(1)}, bf16[2,2,42,8,128]{4,3,2,1,0:T(8,128)(2,1)S(1)}, u32[]{:S(2)}, u32[]{:S(2)}) collective-permute-start(bf16[2,2,42,8,128]{4,3,2,1,0:T(8,128)(2,1)S(1)} %get-tuple-element.47), channel_id=1, source_target_pairs={{0,16},{8,24},{16,0},{24,8},{1,17},{9,25},{17,1},{25,9},{2,18},{10... | collective-permute-start | bytes 1032200 | tf_op jit(solution)/shard_map/ppermute | solution.py:531
  43.6 17.0 %collective-permute-start.8 = (bf16[2,2,42,8,128]{4,3,2,1,0:T(8,128)(2,1)S(1)}, bf16[2,2,42,8,128]{4,3,2,1,0:T(8,128)(2,1)S(1)}, u32[]{:S(2)}, u32[]{:S(2)}) collective-permute-start(bf16[2,2,42,8,128]{4,3,2,1,0:T(8,128)(2,1)S(1)} %get-tuple-element.47), channel_id=1, source_target_pairs={{0,8},{8,0},{16,24},{24,16},{1,9},{9,1},{17,25},{25,17},{2,10},{10... | collective-permute-start | bytes 1032200 | tf_op jit(solution)/shard_map/ppermute | solution.py:527
  49.8 14.6 %collective-permute-start.27 = (bf16[2,120,8,128]{3,2,1,0:T(8,128)(2,1)S(1)}, bf16[2,120,8,128]{3,2,1,0:T(8,128)(2,1)S(1)}, u32[]{:S(2)}, u32[]{:S(2)}) collective-permute-start(bf16[2,120,8,128]{3,2,1,0:T(8,128)(2,1)S(1)} %collective-permute-done.26), channel_id=1, source_target_pairs={{2,0},{3,1},{4,2},{5,3},{10,8},{11,9},{12,10},{13,11},{18,16},{19,... | collective-permute-start | bytes 1474568 | tf_op jit(solution)/shard_map/ppermute | solution.py:567
  67.9 17.7 %collective-permute-start.13 = (bf16[4,4,2,2,8,128]{5,4,3,2,1,0:T(8,128)(2,1)S(1)}, bf16[4,4,2,2,8,128]{5,4,3,2,1,0:T(8,128)(2,1)S(1)}, u32[]{:S(2)}, u32[]{:S(2)}) collective-permute-start(bf16[4,4,2,2,8,128]{5,4,3,2,1,0:T(8,128)(2,1)S(1)} %copy.152), channel_id=1, source_target_pairs={{0,1},{1,0},{2,3},{3,2},{4,5},{5,4},{6,7},{7,6},{8,9},{9,8},{10,11... | collective-permute-start | bytes 393224 | tf_op jit(solution)/shard_map/ppermute | solution.py:535
  69.5 77.7 %collective-permute-start.14 = (bf16[1280,8,128]{2,1,0:T(8,128)(2,1)}, bf16[1280,8,128]{2,1,0:T(8,128)(2,1)}, u32[]{:S(2)}, u32[]{:S(2)}) collective-permute-start(bf16[1280,8,128]{2,1,0:T(8,128)(2,1)} %bitcast.48), channel_id=1, source_target_pairs={{0,1},{1,0},{2,3},{3,2},{4,5},{5,4},{6,7},{7,6},{8,9},{9,8},{10,11... | collective-permute-start | bytes 7864328 | tf_op jit(solution)/shard_map/ppermute | solution.py:535
  83.5 24.9 %collective-permute-start.32 = (bf16[2,2,120,8,128]{4,3,2,1,0:T(8,128)(2,1)}, bf16[2,2,120,8,128]{4,3,2,1,0:T(8,128)(2,1)S(1)}, u32[]{:S(2)}, u32[]{:S(2)}) collective-permute-start(bf16[2,2,120,8,128]{4,3,2,1,0:T(8,128)(2,1)} %get-tuple-element.24), channel_id=1, source_target_pairs={{0,16},{8,24},{16,0},{24,8},{1,17},{9,25},{17,1},{25,9},{2,18},{10... | collective-permute-start | bytes 2949128 | tf_op jit(solution)/shard_map/ppermute | solution.py:531
  85.1 25.0 %collective-permute-start.29 = (bf16[2,2,120,8,128]{4,3,2,1,0:T(8,128)(2,1)}, bf16[2,2,120,8,128]{4,3,2,1,0:T(8,128)(2,1)}, u32[]{:S(2)}, u32[]{:S(2)}) collective-permute-start(bf16[2,2,120,8,128]{4,3,2,1,0:T(8,128)(2,1)} %get-tuple-element.26), channel_id=1, source_target_pairs={{0,8},{8,0},{16,24},{24,16},{1,9},{9,1},{17,25},{25,17},{2,10},{10... | collective-permute-start | bytes 2949128 | tf_op jit(solution)/shard_map/ppermute | solution.py:527
  85.7 45.5 %collective-permute-start.30 = (bf16[2,2,120,8,128]{4,3,2,1,0:T(8,128)(2,1)}, bf16[2,2,120,8,128]{4,3,2,1,0:T(8,128)(2,1)}, u32[]{:S(2)}, u32[]{:S(2)}) collective-permute-start(bf16[2,2,120,8,128]{4,3,2,1,0:T(8,128)(2,1)} %get-tuple-element.24), channel_id=1, source_target_pairs={{0,8},{8,0},{16,24},{24,16},{1,9},{9,1},{17,25},{25,17},{2,10},{10... | collective-permute-start | bytes 2949128 | tf_op jit(solution)/shard_map/ppermute | solution.py:527
  88.6 44.9 %collective-permute-start.31 = (bf16[2,2,120,8,128]{4,3,2,1,0:T(8,128)(2,1)}, bf16[2,2,120,8,128]{4,3,2,1,0:T(8,128)(2,1)S(1)}, u32[]{:S(2)}, u32[]{:S(2)}) collective-permute-start(bf16[2,2,120,8,128]{4,3,2,1,0:T(8,128)(2,1)} %get-tuple-element.26), channel_id=1, source_target_pairs={{0,16},{8,24},{16,0},{24,8},{1,17},{9,25},{17,1},{25,9},{2,18},{10... | collective-permute-start | bytes 2949128 | tf_op jit(solution)/shard_map/ppermute | solution.py:531
  108.4 37.7 %collective-permute-start.34 = (bf16[2,2,120,8,128]{4,3,2,1,0:T(8,128)(2,1)S(1)}, bf16[2,2,120,8,128]{4,3,2,1,0:T(8,128)(2,1)S(1)}, u32[]{:S(2)}, u32[]{:S(2)}) collective-permute-start(bf16[2,2,120,8,128]{4,3,2,1,0:T(8,128)(2,1)S(1)} %collective-permute-done.32), channel_id=1, source_target_pairs={{0,8},{8,0},{16,24},{24,16},{1,9},{9,1},{17,25},{25,17},{2,10},{10... | collective-permute-start | bytes 2949128 | tf_op jit(solution)/shard_map/ppermute | solution.py:527
  110.2 34.6 %collective-permute-start.33 = (bf16[2,2,120,8,128]{4,3,2,1,0:T(8,128)(2,1)}, bf16[2,2,120,8,128]{4,3,2,1,0:T(8,128)(2,1)S(1)}, u32[]{:S(2)}, u32[]{:S(2)}) collective-permute-start(bf16[2,2,120,8,128]{4,3,2,1,0:T(8,128)(2,1)} %collective-permute-done.29), channel_id=1, source_target_pairs={{0,16},{8,24},{16,0},{24,8},{1,17},{9,25},{17,1},{25,9},{2,18},{10... | collective-permute-start | bytes 2949128 | tf_op jit(solution)/shard_map/ppermute | solution.py:531
  147.1 83.8 %collective-permute-start.35 = (bf16[3840,8,128]{2,1,0:T(8,128)(2,1)}, bf16[3840,8,128]{2,1,0:T(8,128)(2,1)}, u32[]{:S(2)}, u32[]{:S(2)}) collective-permute-start(bf16[3840,8,128]{2,1,0:T(8,128)(2,1)} %bitcast.121), channel_id=1, source_target_pairs={{0,1},{1,0},{2,3},{3,2},{4,5},{5,4},{6,7},{7,6},{8,9},{9,8},{10,11... | collective-permute-start | bytes 23592968 | tf_op jit(solution)/shard_map/ppermute | solution.py:535
  283.5 14.8 %collective-permute-start.36 = (bf16[4,192,640]{2,1,0:T(8,128)(2,1)S(1)}, bf16[4,192,640]{2,1,0:T(8,128)(2,1)}, u32[]{:S(2)}, u32[]{:S(2)}) collective-permute-start(bf16[4,192,640]{2,1,0:T(8,128)(2,1)S(1)} %copy-done.6), channel_id=1, source_target_pairs={{0,1},{1,0},{2,3},{3,2},{4,5},{5,4},{6,7},{7,6},{8,9},{9,8},{10,11... | collective-permute-start | bytes 2949128 | tf_op jit(solution)/shard_map/ppermute | solution.py:535
  295.8 63.7 %collective-permute-start.57 = (bf16[3840,8,128]{2,1,0:T(8,128)(2,1)}, bf16[3840,8,128]{2,1,0:T(8,128)(2,1)}, u32[]{:S(2)}, u32[]{:S(2)}) collective-permute-start(bf16[3840,8,128]{2,1,0:T(8,128)(2,1)} %pad_maximum_fusion), channel_id=1, source_target_pairs={{0,1},{1,0},{2,3},{3,2},{4,5},{5,4},{6,7},{7,6},{8,9},{9,8},{10,11... | collective-permute-start | bytes 23592968 | tf_op jit(solution)/shard_map/ppermute | solution.py:535
  353.9 37.8 %collective-permute-start.43 = (bf16[4,4,2,42,8,128]{5,4,3,2,1,0:T(8,128)(2,1)S(1)}, bf16[4,4,2,42,8,128]{5,4,3,2,1,0:T(8,128)(2,1)S(1)}, u32[]{:S(2)}, u32[]{:S(2)}) collective-permute-start(bf16[4,4,2,42,8,128]{5,4,3,2,1,0:T(8,128)(2,1)S(1)} %pad_maximum_fusion.1), channel_id=1, source_target_pairs={{0,1},{1,0},{2,3},{3,2},{4,5},{5,4},{6,7},{7,6},{8,9},{9,8},{10,11... | collective-permute-start | bytes 8257544 | tf_op jit(solution)/shard_map/ppermute | solution.py:535
  390.0 24.8 %collective-permute-start.61 = (bf16[2,2,120,8,128]{4,3,2,1,0:T(8,128)(2,1)S(1)}, bf16[2,2,120,8,128]{4,3,2,1,0:T(8,128)(2,1)S(1)}, u32[]{:S(2)}, u32[]{:S(2)}) collective-permute-start(bf16[2,2,120,8,128]{4,3,2,1,0:T(8,128)(2,1)S(1)} %get-tuple-element.29), channel_id=1, source_target_pairs={{0,16},{8,24},{16,0},{24,8},{1,17},{9,25},{17,1},{25,9},{2,18},{10... | collective-permute-start | bytes 2949128 | tf_op jit(solution)/shard_map/ppermute | solution.py:531
  392.6 29.6 %collective-permute-start.47 = (bf16[2,2,42,8,128]{4,3,2,1,0:T(8,128)(2,1)S(1)}, bf16[2,2,42,8,128]{4,3,2,1,0:T(8,128)(2,1)S(1)}, u32[]{:S(2)}, u32[]{:S(2)}) collective-permute-start(bf16[2,2,42,8,128]{4,3,2,1,0:T(8,128)(2,1)S(1)} %get-tuple-element.37), channel_id=1, source_target_pairs={{0,16},{8,24},{16,0},{24,8},{1,17},{9,25},{17,1},{25,9},{2,18},{10... | collective-permute-start | bytes 1032200 | tf_op jit(solution)/shard_map/ppermute | solution.py:531
  394.0 62.8 %collective-permute-start.59 = (bf16[2,2,120,8,128]{4,3,2,1,0:T(8,128)(2,1)S(1)}, bf16[2,2,120,8,128]{4,3,2,1,0:T(8,128)(2,1)S(1)}, u32[]{:S(2)}, u32[]{:S(2)}) collective-permute-start(bf16[2,2,120,8,128]{4,3,2,1,0:T(8,128)(2,1)S(1)} %get-tuple-element.30), channel_id=1, source_target_pairs={{0,8},{8,0},{16,24},{24,16},{1,9},{9,1},{17,25},{25,17},{2,10},{10... | collective-permute-start | bytes 2949128 | tf_op jit(solution)/shard_map/ppermute | solution.py:527
  395.5 62.8 %collective-permute-start.63 = (bf16[2,2,120,8,128]{4,3,2,1,0:T(8,128)(2,1)S(1)}, bf16[2,2,120,8,128]{4,3,2,1,0:T(8,128)(2,1)S(1)}, u32[]{:S(2)}, u32[]{:S(2)}) collective-permute-start(bf16[2,2,120,8,128]{4,3,2,1,0:T(8,128)(2,1)S(1)} %get-tuple-element.32), channel_id=1, source_target_pairs={{0,16},{8,24},{16,0},{24,8},{1,17},{9,25},{17,1},{25,9},{2,18},{10... | collective-permute-start | bytes 2949128 | tf_op jit(solution)/shard_map/ppermute | solution.py:531
  415.1 43.2 %collective-permute-start.62 = (bf16[2,2,120,8,128]{4,3,2,1,0:T(8,128)(2,1)S(1)}, bf16[2,2,120,8,128]{4,3,2,1,0:T(8,128)(2,1)S(1)}, u32[]{:S(2)}, u32[]{:S(2)}) collective-permute-start(bf16[2,2,120,8,128]{4,3,2,1,0:T(8,128)(2,1)S(1)} %fusion.37), channel_id=1, source_target_pairs={{0,8},{8,0},{16,24},{24,16},{1,9},{9,1},{17,25},{25,17},{2,10},{10... | collective-permute-start | bytes 2949128 | tf_op jit(solution)/shard_map/ppermute | solution.py:527
  416.6 28.1 %collective-permute-start.45 = (bf16[2,2,42,8,128]{4,3,2,1,0:T(8,128)(2,1)S(1)}, bf16[2,2,42,8,128]{4,3,2,1,0:T(8,128)(2,1)S(1)}, u32[]{:S(2)}, u32[]{:S(2)}) collective-permute-start(bf16[2,2,42,8,128]{4,3,2,1,0:T(8,128)(2,1)S(1)} %get-tuple-element.38), channel_id=1, source_target_pairs={{0,8},{8,0},{16,24},{24,16},{1,9},{9,1},{17,25},{25,17},{2,10},{10... | collective-permute-start | bytes 1032200 | tf_op jit(solution)/shard_map/ppermute | solution.py:527
  422.2 26.6 %collective-permute-start.49 = (bf16[2,2,42,8,128]{4,3,2,1,0:T(8,128)(2,1)S(1)}, bf16[2,2,42,8,128]{4,3,2,1,0:T(8,128)(2,1)S(1)}, u32[]{:S(2)}, u32[]{:S(2)}) collective-permute-start(bf16[2,2,42,8,128]{4,3,2,1,0:T(8,128)(2,1)S(1)} %get-tuple-element.40), channel_id=1, source_target_pairs={{0,16},{8,24},{16,0},{24,8},{1,17},{9,25},{17,1},{25,9},{2,18},{10... | collective-permute-start | bytes 1032200 | tf_op jit(solution)/shard_map/ppermute | solution.py:531
  456.8 23.9 %collective-permute-start.58 = (bf16[2,2,120,8,128]{4,3,2,1,0:T(8,128)(2,1)S(1)}, bf16[2,2,120,8,128]{4,3,2,1,0:T(8,128)(2,1)S(1)}, u32[]{:S(2)}, u32[]{:S(2)}) collective-permute-start(bf16[2,2,120,8,128]{4,3,2,1,0:T(8,128)(2,1)S(1)} %get-tuple-element.31), channel_id=1, source_target_pairs={{0,8},{8,0},{16,24},{24,16},{1,9},{9,1},{17,25},{25,17},{2,10},{10... | collective-permute-start | bytes 2949128 | tf_op jit(solution)/shard_map/ppermute | solution.py:527
  458.9 21.8 %collective-permute-start.60 = (bf16[2,2,120,8,128]{4,3,2,1,0:T(8,128)(2,1)S(1)}, bf16[2,2,120,8,128]{4,3,2,1,0:T(8,128)(2,1)S(1)}, u32[]{:S(2)}, u32[]{:S(2)}) collective-permute-start(bf16[2,2,120,8,128]{4,3,2,1,0:T(8,128)(2,1)S(1)} %get-tuple-element.28), channel_id=1, source_target_pairs={{0,16},{8,24},{16,0},{24,8},{1,17},{9,25},{17,1},{25,9},{2,18},{10... | collective-permute-start | bytes 2949128 | tf_op jit(solution)/shard_map/ppermute | solution.py:531
  466.6 19.6 %collective-permute-start.50 = (bf16[2,42,8,128]{3,2,1,0:T(8,128)(2,1)S(1)}, bf16[2,42,8,128]{3,2,1,0:T(8,128)(2,1)S(1)}, u32[]{:S(2)}, u32[]{:S(2)}) collective-permute-start(bf16[2,42,8,128]{3,2,1,0:T(8,128)(2,1)S(1)} %get-tuple-element.81), channel_id=1, source_target_pairs={{0,2},{1,3},{8,10},{9,11},{16,18},{17,19},{24,26},{25,27}} | collective-permute-start | bytes 516104 | tf_op jit(solution)/shard_map/ppermute | solution.py:622
  470.5 15.7 %collective-permute-start.53 = (bf16[2,42,8,128]{3,2,1,0:T(8,128)(2,1)S(1)}, bf16[2,42,8,128]{3,2,1,0:T(8,128)(2,1)S(1)}, u32[]{:S(2)}, u32[]{:S(2)}) collective-permute-start(bf16[2,42,8,128]{3,2,1,0:T(8,128)(2,1)S(1)} %get-tuple-element.82), channel_id=1, source_target_pairs={{6,4},{7,5},{14,12},{15,13},{22,20},{23,21},{30,28},{31,29}} | collective-permute-start | bytes 516104 | tf_op jit(solution)/shard_map/ppermute | solution.py:624
  481.5 21.6 %collective-permute-start.64 = (bf16[2,120,8,128]{3,2,1,0:T(8,128)(2,1)S(1)}, bf16[2,120,8,128]{3,2,1,0:T(8,128)(2,1)S(1)}, u32[]{:S(2)}, u32[]{:S(2)}) collective-permute-start(bf16[2,120,8,128]{3,2,1,0:T(8,128)(2,1)S(1)} %get-tuple-element.45), channel_id=1, source_target_pairs={{0,2},{1,3},{8,10},{9,11},{16,18},{17,19},{24,26},{25,27}} | collective-permute-start | bytes 1474568 | tf_op jit(solution)/shard_map/ppermute | solution.py:622
  485.5 17.7 %collective-permute-start.67 = (bf16[2,120,8,128]{3,2,1,0:T(8,128)(2,1)S(1)}, bf16[2,120,8,128]{3,2,1,0:T(8,128)(2,1)S(1)}, u32[]{:S(2)}, u32[]{:S(2)}) collective-permute-start(bf16[2,120,8,128]{3,2,1,0:T(8,128)(2,1)S(1)} %get-tuple-element.46), channel_id=1, source_target_pairs={{6,4},{7,5},{14,12},{15,13},{22,20},{23,21},{30,28},{31,29}} | collective-permute-start | bytes 1474568 | tf_op jit(solution)/shard_map/ppermute | solution.py:624
  515.8 14.0 %collective-permute-start.66 = (bf16[2,120,8,128]{3,2,1,0:T(8,128)(2,1)S(1)}, bf16[2,120,8,128]{3,2,1,0:T(8,128)(2,1)S(1)}, u32[]{:S(2)}, u32[]{:S(2)}) collective-permute-start(bf16[2,120,8,128]{3,2,1,0:T(8,128)(2,1)S(1)} %get-tuple-element.41), channel_id=1, source_target_pairs={{0,2},{1,3},{2,4},{3,5},{4,6},{5,7},{8,10},{9,11},{10,12},{11,13},... | collective-permute-start | bytes 1474568 | tf_op jit(solution)/shard_map/ppermute | solution.py:622
  (105 other events, 886.3 us)
